TPU v7x, 512 devices: a whole 4x8x8 slice. The times are simulated.
512 devices in a mesh: ctx: 128 (over y_lo, x, z), mp: 4 (over y_hi, core).
Axes of the slice: x: 4, y: 8 (y_hi: 2, y_lo: 4; y = y_hi * 4 + y_lo), z: 8, core: 2. Of those that a mesh axis runs over, the one named last changes fastest.
Arguments:
- query_rows: bfloat16 [16384, 2048], P('ctx', 'mp'), may hold values from -51 to 51
- key_rows: bfloat16 [16384, 2048], P('ctx', 'mp'), may hold values from -4 to 4
- value_rows: bfloat16 [16384, 2048], P('ctx', 'mp'), may hold values from -6 to 6
- inputs: bfloat16 [16384, 2048], P('ctx', 'mp'), may hold values from -3 to 3
- out_weight: bfloat16 [2048, 2048], P('mp'), may hold values from -0.125 to 0.125
- kernel: float32 [31, 2048], P(None, 'mp'), may hold values from -1 to 1
- cotangent: bfloat16 [16384, 2048], P('ctx', 'mp'), may hold values from -6 to 6
Outputs:
- output: bfloat16 [16384, 2048], P('ctx', 'mp')
- grad_input: bfloat16 [16384, 2048], P('ctx', 'mp')
- grad_query: bfloat16 [16384, 2048], P('ctx', 'mp')
- grad_key: bfloat16 [16384, 2048], P('ctx', 'mp')
- grad_value: bfloat16 [16384, 2048], P('ctx', 'mp')
All inputs are finite; a program needn't handle non-finite values.
Results may differ from a plain program's by a relative error of at most 0.024.
Values may be sent and summed in bfloat16 or wider, within the bound.
A program may use at most 64 MiB of HBM per device.

v0:
```python
import math

import jax
import jax.numpy as jnp
from jax import lax
from jax.sharding import PartitionSpec as P

HDIM = 128
LOOK = 2


def shifted(block, axis, distance):
    devices = range(lax.axis_size(axis))
    route = [(i - distance, i) for i in devices if i - distance in devices]
    return lax.ppermute(block, axis, route)


def with_halo(block, sides, width):
    for axis, dim in sides:
        count = lax.axis_size(axis)
        forward = [(i, i + 1) for i in range(count - 1)]
        backward = [(target, source) for source, target in forward]
        low = lax.ppermute(
            lax.slice_in_dim(block, block.shape[dim] - width, None, axis=dim), axis, forward
        )
        high = lax.ppermute(lax.slice_in_dim(block, 0, width, axis=dim), axis, backward)
        block = jnp.concatenate([low, block, high], axis=dim)
    return block


def kv_move(kv_pair, offset):
    return shifted(kv_pair, "ctx", offset)


def grad_move(part_pair, offset):
    return shifted(part_pair.astype(jnp.bfloat16), "ctx", offset).astype(part_pair.dtype)


def conv_rim(field_rows, rim_width):
    return with_halo(field_rows, (("ctx", 0),), rim_width)


def relay_window(center, move_step):
    lower_list = []
    upper_list = []
    rising = center
    falling = center
    for offset in range(LOOK):
        rising = move_step(rising, 1)
        falling = move_step(falling, -1)
        lower_list.append(rising)
        upper_list.append(falling)
    return lower_list[::-1] + [center] + upper_list


def per_device(query_rows, key_rows, value_rows, inputs, out_weight, kernel, cotangent):
    frames, local_width = query_rows.shape
    local_heads = local_width // HDIM
    score_scale = 1.0 / math.sqrt(HDIM)
    window_len = (2 * LOOK + 1) * frames
    dev_index = lax.axis_index("ctx")
    dev_count = lax.axis_size("ctx")
    owners = dev_index + jnp.arange(window_len, dtype=jnp.int32) // frames - LOOK
    in_range = (owners >= 0) & (owners < dev_count)
    kv_center = jnp.stack([key_rows, value_rows])
    kv_blocks = relay_window(kv_center, kv_move)
    kv_window = jnp.concatenate(kv_blocks, axis=1)
    key_win = kv_window[0].reshape(window_len, local_heads, HDIM)
    value_win = kv_window[1].reshape(window_len, local_heads, HDIM)
    query_heads = query_rows.reshape(frames, local_heads, HDIM)
    scores = (
        jnp.einsum("qhd,khd->hqk", query_heads, key_win, preferred_element_type=jnp.float32)
        * score_scale
    )
    scores = jnp.where(in_range[None, None, :], scores, -jnp.inf)
    row_max = jnp.max(scores, axis=2)
    log_total = row_max + jnp.log(jnp.sum(jnp.exp(scores - row_max[:, :, None]), axis=2))
    attn_probs = jnp.exp(scores - log_total[:, :, None])
    probs_low = attn_probs.astype(jnp.bfloat16)
    attended = jnp.einsum(
        "hqk,khd->qhd", probs_low, value_win, preferred_element_type=jnp.float32
    ).astype(jnp.bfloat16)
    attended_flat = attended.reshape(frames, local_width)
    partial_out = jnp.dot(attended_flat, out_weight, preferred_element_type=jnp.float32)
    mixed = lax.psum_scatter(
        partial_out.astype(jnp.bfloat16), "mp", scatter_dimension=1, tiled=True
    ).astype(jnp.float32)
    hidden = (inputs.astype(jnp.float32) + mixed).astype(jnp.bfloat16)
    taps = kernel.shape[0]
    half_kernel = taps // 2
    hidden_pad = conv_rim(hidden, half_kernel).astype(jnp.float32)
    conv_out = jnp.zeros((frames, local_width), jnp.float32)
    for tap_index in range(taps):
        conv_out = (
            conv_out + kernel[tap_index][None, :] * hidden_pad[tap_index : tap_index + frames]
        )
    conv_gate = jax.nn.sigmoid(conv_out)
    output = (hidden.astype(jnp.float32) + conv_out * conv_gate).astype(jnp.bfloat16)
    grad_conv = (
        cotangent.astype(jnp.float32) * (conv_gate + conv_out * conv_gate * (1.0 - conv_gate))
    ).astype(jnp.bfloat16)
    grad_pad = conv_rim(grad_conv, half_kernel).astype(jnp.float32)
    grad_hidden = cotangent.astype(jnp.float32)
    for tap_index in range(taps):
        first_row = 2 * half_kernel - tap_index
        grad_hidden = (
            grad_hidden + kernel[tap_index][None, :] * grad_pad[first_row : first_row + frames]
        )
    grad_input = grad_hidden.astype(jnp.bfloat16)
    upstream = jnp.einsum(
        "rn,wn->rw",
        lax.all_gather(grad_input, "mp", axis=1, tiled=True),
        out_weight,
        preferred_element_type=jnp.float32,
    ).astype(jnp.bfloat16)
    up_heads = upstream.reshape(frames, local_heads, HDIM)
    row_delta = jnp.sum(up_heads.astype(jnp.float32) * attended.astype(jnp.float32), axis=2).T
    grad_dots = jnp.einsum("qhd,khd->hqk", up_heads, value_win, preferred_element_type=jnp.float32)
    grad_scores = (attn_probs * (grad_dots - row_delta[:, :, None]) * score_scale).astype(
        jnp.bfloat16
    )
    grad_query = jnp.einsum(
        "hqk,khd->qhd", grad_scores, key_win, preferred_element_type=jnp.float32
    )
    grad_query = grad_query.astype(jnp.bfloat16).reshape(frames, local_width)
    key_parts = jnp.einsum(
        "hqk,qhd->khd", grad_scores, query_heads, preferred_element_type=jnp.float32
    )
    value_parts = jnp.einsum(
        "hqk,qhd->khd", probs_low, up_heads, preferred_element_type=jnp.float32
    )
    part_stack = jnp.stack(
        [key_parts.reshape(window_len, local_width), value_parts.reshape(window_len, local_width)]
    )

    def part_block(position):
        return part_stack[:, position * frames : (position + 1) * frames]

    rising = part_block(2 * LOOK)
    offset = 1
    rising = grad_move(rising, 1) + part_block(LOOK + offset)
    rising = grad_move(rising, 1)
    falling = part_block(0)
    offset = 1
    falling = grad_move(falling, -1) + part_block(LOOK - offset)
    falling = grad_move(falling, -1)
    key_sums = part_block(LOOK) + rising + falling
    grad_key = key_sums[0].astype(jnp.bfloat16)
    grad_value = key_sums[1].astype(jnp.bfloat16)
    return (output, grad_input, grad_query, grad_key, grad_value)


def solution(mesh):
    placed = (
        P("ctx", "mp"),
        P("ctx", "mp"),
        P("ctx", "mp"),
        P("ctx", "mp"),
        P("mp", None),
        P(None, "mp"),
        P("ctx", "mp"),
    )
    return jax.shard_map(
        per_device,
        mesh=mesh,
        in_specs=placed,
        out_specs=(P("ctx", "mp"), P("ctx", "mp"), P("ctx", "mp"), P("ctx", "mp"), P("ctx", "mp")),
        check_vma=False,
    )
```

profile of v0, /device:TPU:9, one launch (start us, length us, event | category | flops | bytes accessed | tf_op | source)
XLA Modules:
  0.0 187.7 jit_solution(1581389626179336944)
XLA Ops:
  7.2 0.0 copy-start
  7.2 0.0 reduce-scatter.2.cloned.1.call-start
  7.2 1.2 copy.27
  8.4 1.0 copy.28
  9.5 4.0 %collective-permute-start = (bf16[2,128,512]{1,2,0:T(8,128)(2,1)S(1)}, bf16[2,128,512]{1,2,0:T(8,128)(2,1)S(1)}, u32[]{:S(2)}, u32[]{:S(2)}) collective-permute-start(bf16[2,128,512]{1,2,0:T(8,128)(2,1)S(1)} %pad_maximum_fusion.1), channel_id=1, source_target_pairs={{0,4},{4,8},{8,12},{12,16},{16,20},{20,24},{24,28},{28,32},{32,36}... | collective-permute-start | bytes 786440 | tf_op jit(solution)/shard_map/ppermute | solution.py:15
  13.5 10.7 %collective-permute-start.2 = (bf16[2,128,512]{1,2,0:T(8,128)(2,1)S(1)}, bf16[2,128,512]{1,2,0:T(8,128)(2,1)S(1)}, u32[]{:S(2)}, u32[]{:S(2)}) collective-permute-start(bf16[2,128,512]{1,2,0:T(8,128)(2,1)S(1)} %pad_maximum_fusion.1), channel_id=1, source_target_pairs={{4,0},{8,4},{12,8},{16,12},{20,16},{24,20},{28,24},{32,28},{36,32}... | collective-permute-start | bytes 786440 | tf_op jit(solution)/shard_map/ppermute | solution.py:15
  24.1 4.1 %collective-permute-done = bf16[2,128,512]{1,2,0:T(8,128)(2,1)S(1)} collective-permute-done((bf16[2,128,512]{1,2,0:T(8,128)(2,1)S(1)}, bf16[2,128,512]{1,2,0:T(8,128)(2,1)S(1)}, u32[]{:S(2)}, u32[]{:S(2)}) %collective-permute-start) | collective-permute-done | bytes 262176 | tf_op jit(solution)/shard_map/ppermute | solution.py:15
  28.2 1.9 %collective-permute-start.1 = (bf16[2,128,512]{1,2,0:T(8,128)(2,1)S(1)}, bf16[2,128,512]{1,2,0:T(8,128)(2,1)S(1)}, u32[]{:S(2)}, u32[]{:S(2)}) collective-permute-start(bf16[2,128,512]{1,2,0:T(8,128)(2,1)S(1)} %collective-permute-done), channel_id=1, source_target_pairs={{0,4},{4,8},{8,12},{12,16},{16,20},{20,24},{24,28},{28,32},{32,36}... | collective-permute-start | bytes 786440 | tf_op jit(solution)/shard_map/ppermute | solution.py:15
  30.2 1.0 copy.51
  31.2 0.0 copy-start.9
  31.2 7.6 %collective-permute-start.3 = (bf16[2,128,512]{1,2,0:T(8,128)(2,1)S(1)}, bf16[2,128,512]{1,2,0:T(8,128)(2,1)S(1)}, u32[]{:S(2)}, u32[]{:S(2)}) collective-permute-start(bf16[2,128,512]{1,2,0:T(8,128)(2,1)S(1)} %collective-permute-done.2), channel_id=1, source_target_pairs={{4,0},{8,4},{12,8},{16,12},{20,16},{24,20},{28,24},{32,28},{36,32}... | collective-permute-start | bytes 786440 | tf_op jit(solution)/shard_map/ppermute | solution.py:15
  38.8 2.1 %collective-permute-done.1 = bf16[2,128,512]{1,2,0:T(8,128)(2,1)S(1)} collective-permute-done((bf16[2,128,512]{1,2,0:T(8,128)(2,1)S(1)}, bf16[2,128,512]{1,2,0:T(8,128)(2,1)S(1)}, u32[]{:S(2)}, u32[]{:S(2)}) %collective-permute-start.1) | collective-permute-done | bytes 262176 | tf_op jit(solution)/shard_map/ppermute | solution.py:15
  41.0 0.1 constant_dynamic-update-slice_fusion.3
  41.0 0.1 constant_dynamic-update-slice_fusion.2
  41.1 0.1 constant_dynamic-update-slice_fusion.1
  41.2 1.7 collective-permute-done.3
  42.9 0.1 constant_dynamic-update-slice_fusion
  42.9 0.1 fusion.93
  43.1 0.5 fusion.98
  43.6 0.2 exponential_reduce_fusion
  43.8 0.1 copy-done.2
  43.9 0.2 copy-done.4
  44.1 0.4 convolution_convert_fusion.3
  44.5 0.0 copy-start.11
  44.5 0.6 copy-done.11
  45.2 1.3 convolution_convert_fusion
  46.4 0.0 reduce-scatter.2.cloned.1.call-update
  46.5 1.8 fusion.96
  48.2 43.9 %reduce-scatter.2.cloned.1.call-done = bf16[128,512]{1,0:T(8,128)(2,1)} async-done(((bf16[128,2048]{1,0:T(8,128)(2,1)}), bf16[128,512]{1,0:T(8,128)(2,1)}) %reduce-scatter.2.cloned.1.call-update) | async-done | bytes 131088 | tf_op jit(solution)/shard_map/reduce_scatter | solution.py:85
  92.2 1.0 add_convert_fusion.1
  93.2 3.3 %collective-permute-start.4 = (bf16[15,512]{1,0:T(8,128)(2,1)S(1)}, bf16[15,512]{1,0:T(8,128)(2,1)S(1)}, u32[]{:S(2)}, u32[]{:S(2)}) collective-permute-start(bf16[15,512]{1,0:T(8,128)(2,1)S(1)} %get-tuple-element.27), channel_id=1, source_target_pairs={{0,4},{4,8},{8,12},{12,16},{16,20},{20,24},{24,28},{28,32},{32,36}... | collective-permute-start | bytes 46088 | tf_op jit(solution)/shard_map/ppermute | solution.py:23
  96.5 6.2 %collective-permute-start.5 = (bf16[15,512]{1,0:T(8,128)(2,1)S(1)}, bf16[15,512]{1,0:T(8,128)(2,1)S(1)}, u32[]{:S(2)}, u32[]{:S(2)}) collective-permute-start(bf16[15,512]{1,0:T(8,128)(2,1)S(1)} %get-tuple-element.28), channel_id=1, source_target_pairs={{4,0},{8,4},{12,8},{16,12},{20,16},{24,20},{28,24},{32,28},{36,32}... | collective-permute-start | bytes 46088 | tf_op jit(solution)/shard_map/ppermute | solution.py:26
  102.7 1.0 fusion.97
  103.8 0.0 copy-start.15
  104.0 2.3 %fusion.17 = (bf16[128,512]{1,0:T(8,128)(2,1)S(1)}, f32[128,512]{1,0:T(8,128)}) fusion(bf16[128,512]{1,0:T(8,128)(2,1)S(1)} %copy-done.14, f32[158,512]{1,0:T(8,128)S(1)} %maximum_convert_fusion, f32[512]{0:T(512)S(1)} %bitcast.146, f32[512]{0:T(512)S(1)} %bitcast.148, f32[512]{0:T(512)S(1)} %bitcast.90, f32[512]{0:T(512)S(1)} %bitcast.92, f32[512]{0:T(512)} %bitcast.94, ...), kind=kLoop, calls=%fused_computation.34 | loop fusion | flops 4653056 | bytes 8714240 | tf_op jit(solution)/shard_map/convert_element_type | solution.py:101
  106.3 1.9 %collective-permute-start.6 = (bf16[15,512]{1,0:T(8,128)(2,1)S(1)}, bf16[15,512]{1,0:T(8,128)(2,1)S(1)}, u32[]{:S(2)}, u32[]{:S(2)}) collective-permute-start(bf16[15,512]{1,0:T(8,128)(2,1)S(1)} %get-tuple-element.25), channel_id=1, source_target_pairs={{0,4},{4,8},{8,12},{12,16},{16,20},{20,24},{24,28},{28,32},{32,36}... | collective-permute-start | bytes 46088 | tf_op jit(solution)/shard_map/ppermute | solution.py:23
  108.2 7.7 %collective-permute-start.7 = (bf16[15,512]{1,0:T(8,128)(2,1)S(1)}, bf16[15,512]{1,0:T(8,128)(2,1)S(1)}, u32[]{:S(2)}, u32[]{:S(2)}) collective-permute-start(bf16[15,512]{1,0:T(8,128)(2,1)S(1)} %get-tuple-element.26), channel_id=1, source_target_pairs={{4,0},{8,4},{12,8},{16,12},{20,16},{24,20},{28,24},{32,28},{36,32}... | collective-permute-start | bytes 46088 | tf_op jit(solution)/shard_map/ppermute | solution.py:26
  115.9 0.8 collective-permute-done.7
  116.9 0.8 fusion.44
  117.8 13.8 %all_gather.3 = bf16[128,2048]{1,0:T(8,128)(2,1)S(1)} all-gather(bf16[128,512]{1,0:T(8,128)(2,1)S(1)} %fusion.44), channel_id=1, replica_groups=mesh['ctx'=128,'mp'=4] {'mp'}, dimensions={1}, use_global_device_ids=true | all-gather | bytes 655360 | tf_op jit(solution)/shard_map/all_gather | solution.py:112
  131.6 1.5 convolution_convert_fusion.1
  133.1 1.0 copy.32
  134.1 1.0 multiply_reduce_fusion
  135.1 1.5 fusion.80
  136.6 1.3 fusion.5
  137.9 1.7 copy.41
  139.7 2.5 %fusion.99 = f32[4,640,128]{1,2,0:T(8,128)} fusion(bf16[4,128,640]{1,2,0:T(8,128)(2,1)} %fusion.5, bf16[128,4,128]{0,2,1:T(8,128)(2,1)S(1)} %bitcast.81), kind=kOutput, calls=%fused_computation.194 | convolution fusion | flops 83886080 | bytes 2097152 | tf_op jit(solution)/shard_map/hqk,qhd->khd/dot_general | solution.py:126
  142.2 2.8 %copy.40 = f32[1,640,512]{2,1,0:T(8,128)} copy(f32[1,640,512]{1,2,0:T(8,128)} %bitcast.77) | data formatting | bytes 2621440 | tf_op jit(solution)/shard_map/stack;reshape | solution.py:132
  145.0 1.6 fusion
  146.7 1.9 %collective-permute-start.8 = (bf16[2,128,512]{2,1,0:T(8,128)(2,1)S(1)}, bf16[2,128,512]{2,1,0:T(8,128)(2,1)S(1)}, u32[]{:S(2)}, u32[]{:S(2)}) collective-permute-start(bf16[2,128,512]{2,1,0:T(8,128)(2,1)S(1)} %get-tuple-element.19), channel_id=1, source_target_pairs={{0,4},{4,8},{8,12},{12,16},{16,20},{20,24},{24,28},{28,32},{32,36}... | collective-permute-start | bytes 786440 | tf_op jit(solution)/shard_map/ppermute | solution.py:15
  148.6 0.0 copy-start.8
  148.6 8.6 %collective-permute-start.10 = (bf16[2,128,512]{2,1,0:T(8,128)(2,1)S(1)}, bf16[2,128,512]{2,1,0:T(8,128)(2,1)S(1)}, u32[]{:S(2)}, u32[]{:S(2)}) collective-permute-start(bf16[2,128,512]{2,1,0:T(8,128)(2,1)S(1)} %get-tuple-element.20), channel_id=1, source_target_pairs={{4,0},{8,4},{12,8},{16,12},{20,16},{24,20},{28,24},{32,28},{36,32}... | collective-permute-start | bytes 786440 | tf_op jit(solution)/shard_map/ppermute | solution.py:15
  157.2 4.4 %collective-permute-done.8 = bf16[2,128,512]{2,1,0:T(8,128)(2,1)S(1)} collective-permute-done((bf16[2,128,512]{2,1,0:T(8,128)(2,1)S(1)}, bf16[2,128,512]{2,1,0:T(8,128)(2,1)S(1)}, u32[]{:S(2)}, u32[]{:S(2)}) %collective-permute-start.8) | collective-permute-done | bytes 262176 | tf_op jit(solution)/shard_map/ppermute | solution.py:15
  161.6 1.1 collective-permute-done.10
  162.7 1.0 fusion.13
  163.7 1.9 %collective-permute-start.9 = (bf16[2,128,512]{2,1,0:T(8,128)(2,1)}, bf16[2,128,512]{2,1,0:T(8,128)(2,1)}, u32[]{:S(2)}, u32[]{:S(2)}) collective-permute-start(bf16[2,128,512]{2,1,0:T(8,128)(2,1)} %get-tuple-element.17), channel_id=1, source_target_pairs={{0,4},{4,8},{8,12},{12,16},{16,20},{20,24},{24,28},{28,32},{32,36}... | collective-permute-start | bytes 786440 | tf_op jit(solution)/shard_map/ppermute | solution.py:15
  165.6 8.3 %collective-permute-start.11 = (bf16[2,128,512]{2,1,0:T(8,128)(2,1)}, bf16[2,128,512]{2,1,0:T(8,128)(2,1)}, u32[]{:S(2)}, u32[]{:S(2)}) collective-permute-start(bf16[2,128,512]{2,1,0:T(8,128)(2,1)} %get-tuple-element.18), channel_id=1, source_target_pairs={{4,0},{8,4},{12,8},{16,12},{20,16},{24,20},{28,24},{32,28},{36,32}... | collective-permute-start | bytes 786440 | tf_op jit(solution)/shard_map/ppermute | solution.py:15
  174.0 0.7 add_convert_fusion
  174.7 0.3 convolution_convert_fusion.2
  175.1 0.8 copy.42
  175.8 2.2 %collective-permute-done.9 = bf16[2,128,512]{2,1,0:T(8,128)(2,1)} collective-permute-done((bf16[2,128,512]{2,1,0:T(8,128)(2,1)}, bf16[2,128,512]{2,1,0:T(8,128)(2,1)}, u32[]{:S(2)}, u32[]{:S(2)}) %collective-permute-start.9) | collective-permute-done | bytes 262176 | tf_op jit(solution)/shard_map/ppermute | solution.py:15
  178.0 0.9 collective-permute-done.11
  178.9 1.2 fusion.10
  180.1 0.7 slice_bitcast_fusion
  (67 shorter events, 0.4 us)
Async XLA Ops:
  7.2 38.0 %copy-start = (bf16[512,2048]{1,0:T(8,128)(2,1)S(1)}, bf16[512,2048]{1,0:T(8,128)(2,1)}, u32[]{:S(2)}) copy-start(bf16[512,2048]{1,0:T(8,128)(2,1)} %param.11) | copy-start | bytes 6291460
  7.2 85.0 %reduce-scatter.2.cloned.1.call-start = ((), (), s32[]{:S(2)}) async-start(), calls=%async_computation.1 | async-start | bytes 655360 | tf_op jit(solution)/shard_map/reduce_scatter | solution.py:85
  9.5 18.8 %collective-permute-start = (bf16[2,128,512]{1,2,0:T(8,128)(2,1)S(1)}, bf16[2,128,512]{1,2,0:T(8,128)(2,1)S(1)}, u32[]{:S(2)}, u32[]{:S(2)}) collective-permute-start(bf16[2,128,512]{1,2,0:T(8,128)(2,1)S(1)} %pad_maximum_fusion.1), channel_id=1, source_target_pairs={{0,4},{4,8},{8,12},{12,16},{16,20},{20,24},{24,28},{28,32},{32,36}... | collective-permute-start | bytes 786440 | tf_op jit(solution)/shard_map/ppermute | solution.py:15
  13.5 17.7 %collective-permute-start.2 = (bf16[2,128,512]{1,2,0:T(8,128)(2,1)S(1)}, bf16[2,128,512]{1,2,0:T(8,128)(2,1)S(1)}, u32[]{:S(2)}, u32[]{:S(2)}) collective-permute-start(bf16[2,128,512]{1,2,0:T(8,128)(2,1)S(1)} %pad_maximum_fusion.1), channel_id=1, source_target_pairs={{4,0},{8,4},{12,8},{16,12},{20,16},{24,20},{28,24},{32,28},{36,32}... | collective-permute-start | bytes 786440 | tf_op jit(solution)/shard_map/ppermute | solution.py:15
  28.2 12.7 %collective-permute-start.1 = (bf16[2,128,512]{1,2,0:T(8,128)(2,1)S(1)}, bf16[2,128,512]{1,2,0:T(8,128)(2,1)S(1)}, u32[]{:S(2)}, u32[]{:S(2)}) collective-permute-start(bf16[2,128,512]{1,2,0:T(8,128)(2,1)S(1)} %collective-permute-done), channel_id=1, source_target_pairs={{0,4},{4,8},{8,12},{12,16},{16,20},{20,24},{24,28},{28,32},{32,36}... | collective-permute-start | bytes 786440 | tf_op jit(solution)/shard_map/ppermute | solution.py:15
  31.2 11.9 %copy-start.9 = (bf16[128,512]{0,1:T(8,128)(2,1)}, bf16[128,512]{0,1:T(8,128)(2,1)S(1)}, u32[]{:S(2)}) copy-start(bf16[128,512]{0,1:T(8,128)(2,1)S(1)} %copy.51) | copy-start | bytes 393220
  31.2 11.7 %collective-permute-start.3 = (bf16[2,128,512]{1,2,0:T(8,128)(2,1)S(1)}, bf16[2,128,512]{1,2,0:T(8,128)(2,1)S(1)}, u32[]{:S(2)}, u32[]{:S(2)}) collective-permute-start(bf16[2,128,512]{1,2,0:T(8,128)(2,1)S(1)} %collective-permute-done.2), channel_id=1, source_target_pairs={{4,0},{8,4},{12,8},{16,12},{20,16},{24,20},{28,24},{32,28},{36,32}... | collective-permute-start | bytes 786440 | tf_op jit(solution)/shard_map/ppermute | solution.py:15
  43.1 0.8 copy-start.2
  43.1 1.0 copy-start.4
  44.5 0.7 copy-start.11
  46.4 57.4 %copy-start.14 = (bf16[128,512]{1,0:T(8,128)(2,1)S(1)}, bf16[128,512]{1,0:T(8,128)(2,1)}, u32[]{:S(2)}) copy-start(bf16[128,512]{1,0:T(8,128)(2,1)} %param.13) | copy-start | bytes 393220
  93.2 10.6 %copy-start.7 = (bf16[128,512]{1,0:T(8,128)(2,1)}, bf16[128,512]{1,0:T(8,128)(2,1)S(1)}, u32[]{:S(2)}) copy-start(bf16[128,512]{1,0:T(8,128)(2,1)S(1)} %add_convert_fusion.1) | copy-start | bytes 393220
  93.2 10.5 %collective-permute-start.4 = (bf16[15,512]{1,0:T(8,128)(2,1)S(1)}, bf16[15,512]{1,0:T(8,128)(2,1)S(1)}, u32[]{:S(2)}, u32[]{:S(2)}) collective-permute-start(bf16[15,512]{1,0:T(8,128)(2,1)S(1)} %get-tuple-element.27), channel_id=1, source_target_pairs={{0,4},{4,8},{8,12},{12,16},{16,20},{20,24},{24,28},{28,32},{32,36}... | collective-permute-start | bytes 46088 | tf_op jit(solution)/shard_map/ppermute | solution.py:23
  96.5 7.3 %collective-permute-start.5 = (bf16[15,512]{1,0:T(8,128)(2,1)S(1)}, bf16[15,512]{1,0:T(8,128)(2,1)S(1)}, u32[]{:S(2)}, u32[]{:S(2)}) collective-permute-start(bf16[15,512]{1,0:T(8,128)(2,1)S(1)} %get-tuple-element.28), channel_id=1, source_target_pairs={{4,0},{8,4},{12,8},{16,12},{20,16},{24,20},{28,24},{32,28},{36,32}... | collective-permute-start | bytes 46088 | tf_op jit(solution)/shard_map/ppermute | solution.py:26
  103.8 12.9 %copy-start.15 = (f32[1,512]{1,0:T(1,128)S(1)}, f32[1,512]{1,0:T(1,128)}, u32[]{:S(2)}) copy-start(f32[1,512]{1,0:T(1,128)} %get-tuple-element.32) | copy-start | bytes 6148
  103.8 12.9 %copy-start.16 = (f32[1,512]{1,0:T(1,128)S(1)}, f32[1,512]{1,0:T(1,128)}, u32[]{:S(2)}) copy-start(f32[1,512]{1,0:T(1,128)} %get-tuple-element.33) | copy-start | bytes 6148
  103.8 12.9 %copy-start.17 = (f32[1,512]{1,0:T(1,128)S(1)}, f32[1,512]{1,0:T(1,128)}, u32[]{:S(2)}) copy-start(f32[1,512]{1,0:T(1,128)} %get-tuple-element.34) | copy-start | bytes 6148
  103.9 12.9 %copy-start.18 = (f32[1,512]{1,0:T(1,128)S(1)}, f32[1,512]{1,0:T(1,128)}, u32[]{:S(2)}) copy-start(f32[1,512]{1,0:T(1,128)} %get-tuple-element.35) | copy-start | bytes 6148
  103.9 12.9 %copy-start.19 = (f32[1,512]{1,0:T(1,128)S(1)}, f32[1,512]{1,0:T(1,128)}, u32[]{:S(2)}) copy-start(f32[1,512]{1,0:T(1,128)} %get-tuple-element.36) | copy-start | bytes 6148
  103.9 12.9 %copy-start.20 = (f32[1,512]{1,0:T(1,128)S(1)}, f32[1,512]{1,0:T(1,128)}, u32[]{:S(2)}) copy-start(f32[1,512]{1,0:T(1,128)} %get-tuple-element.37) | copy-start | bytes 6148
  103.9 12.9 %copy-start.21 = (f32[1,512]{1,0:T(1,128)S(1)}, f32[1,512]{1,0:T(1,128)}, u32[]{:S(2)}) copy-start(f32[1,512]{1,0:T(1,128)} %get-tuple-element.38) | copy-start | bytes 6148
  103.9 12.9 %copy-start.22 = (f32[1,512]{1,0:T(1,128)S(1)}, f32[1,512]{1,0:T(1,128)}, u32[]{:S(2)}) copy-start(f32[1,512]{1,0:T(1,128)} %get-tuple-element.39) | copy-start | bytes 6148
  103.9 12.9 %copy-start.23 = (f32[1,512]{1,0:T(1,128)S(1)}, f32[1,512]{1,0:T(1,128)}, u32[]{:S(2)}) copy-start(f32[1,512]{1,0:T(1,128)} %get-tuple-element.40) | copy-start | bytes 6148
  103.9 12.9 %copy-start.24 = (f32[1,512]{1,0:T(1,128)S(1)}, f32[1,512]{1,0:T(1,128)}, u32[]{:S(2)}) copy-start(f32[1,512]{1,0:T(1,128)} %get-tuple-element.41) | copy-start | bytes 6148
  103.9 12.9 %copy-start.25 = (f32[1,512]{1,0:T(1,128)S(1)}, f32[1,512]{1,0:T(1,128)}, u32[]{:S(2)}) copy-start(f32[1,512]{1,0:T(1,128)} %get-tuple-element.42) | copy-start | bytes 6148
  103.9 12.9 %copy-start.26 = (f32[1,512]{1,0:T(1,128)S(1)}, f32[1,512]{1,0:T(1,128)}, u32[]{:S(2)}) copy-start(f32[1,512]{1,0:T(1,128)} %get-tuple-element.43) | copy-start | bytes 6148
  103.9 12.9 %copy-start.27 = (f32[1,512]{1,0:T(1,128)S(1)}, f32[1,512]{1,0:T(1,128)}, u32[]{:S(2)}) copy-start(f32[1,512]{1,0:T(1,128)} %get-tuple-element.44) | copy-start | bytes 6148
  104.0 12.9 %copy-start.28 = (f32[1,512]{1,0:T(1,128)S(1)}, f32[1,512]{1,0:T(1,128)}, u32[]{:S(2)}) copy-start(f32[1,512]{1,0:T(1,128)} %get-tuple-element.45) | copy-start | bytes 6148
  104.0 12.9 %copy-start.29 = (f32[1,512]{1,0:T(1,128)S(1)}, f32[1,512]{1,0:T(1,128)}, u32[]{:S(2)}) copy-start(f32[1,512]{1,0:T(1,128)} %get-tuple-element.46) | copy-start | bytes 6148
  104.0 12.9 %copy-start.30 = (f32[1,512]{1,0:T(1,128)S(1)}, f32[1,512]{1,0:T(1,128)}, u32[]{:S(2)}) copy-start(f32[1,512]{1,0:T(1,128)} %get-tuple-element.47) | copy-start | bytes 6148
  106.3 9.6 %collective-permute-start.6 = (bf16[15,512]{1,0:T(8,128)(2,1)S(1)}, bf16[15,512]{1,0:T(8,128)(2,1)S(1)}, u32[]{:S(2)}, u32[]{:S(2)}) collective-permute-start(bf16[15,512]{1,0:T(8,128)(2,1)S(1)} %get-tuple-element.25), channel_id=1, source_target_pairs={{0,4},{4,8},{8,12},{12,16},{16,20},{20,24},{24,28},{28,32},{32,36}... | collective-permute-start | bytes 46088 | tf_op jit(solution)/shard_map/ppermute | solution.py:23
  108.2 8.5 %collective-permute-start.7 = (bf16[15,512]{1,0:T(8,128)(2,1)S(1)}, bf16[15,512]{1,0:T(8,128)(2,1)S(1)}, u32[]{:S(2)}, u32[]{:S(2)}) collective-permute-start(bf16[15,512]{1,0:T(8,128)(2,1)S(1)} %get-tuple-element.26), channel_id=1, source_target_pairs={{4,0},{8,4},{12,8},{16,12},{20,16},{24,20},{28,24},{32,28},{36,32}... | collective-permute-start | bytes 46088 | tf_op jit(solution)/shard_map/ppermute | solution.py:26
  117.8 13.8 %copy-start.13 = (bf16[128,512]{1,0:T(8,128)(2,1)}, bf16[128,512]{1,0:T(8,128)(2,1)S(1)}, u32[]{:S(2)}) copy-start(bf16[128,512]{1,0:T(8,128)(2,1)S(1)} %fusion.44) | copy-start | bytes 393220
  135.1 1.5 copy-start.5
  137.9 1.8 copy-start.10
  145.0 17.7 %copy-start.1 = (f32[1,640,512]{2,1,0:T(8,128)S(1)}, f32[1,640,512]{2,1,0:T(8,128)}, u32[]{:S(2)}) copy-start(f32[1,640,512]{2,1,0:T(8,128)} %copy.40) | copy-start | bytes 3932164
  146.7 14.9 %collective-permute-start.8 = (bf16[2,128,512]{2,1,0:T(8,128)(2,1)S(1)}, bf16[2,128,512]{2,1,0:T(8,128)(2,1)S(1)}, u32[]{:S(2)}, u32[]{:S(2)}) collective-permute-start(bf16[2,128,512]{2,1,0:T(8,128)(2,1)S(1)} %get-tuple-element.19), channel_id=1, source_target_pairs={{0,4},{4,8},{8,12},{12,16},{16,20},{20,24},{24,28},{28,32},{32,36}... | collective-permute-start | bytes 786440 | tf_op jit(solution)/shard_map/ppermute | solution.py:15
  148.6 25.4 %copy-start.8 = (bf16[128,512]{1,0:T(8,128)(2,1)S(1)}, bf16[128,512]{1,0:T(8,128)(2,1)}, u32[]{:S(2)}) copy-start(bf16[128,512]{1,0:T(8,128)(2,1)} %copy-done.7) | copy-start | bytes 393220
  148.6 25.4 %copy-start.12 = (f32[128,512]{1,0:T(8,128)S(1)}, f32[128,512]{1,0:T(8,128)}, u32[]{:S(2)}) copy-start(f32[128,512]{1,0:T(8,128)} %get-tuple-element.16) | copy-start | bytes 786436
  148.6 26.1 %copy-start.3 = (bf16[1,640,512]{1,2,0:T(8,128)(2,1)S(1)}, bf16[1,640,512]{1,2,0:T(8,128)(2,1)}, u32[]{:S(2)}) copy-start(bf16[1,640,512]{1,2,0:T(8,128)(2,1)} %copy-done.2) | copy-start | bytes 1966084
  148.6 26.1 %copy-start.6 = (bf16[4,128,640]{1,2,0:T(8,128)(2,1)S(1)}, bf16[4,128,640]{1,2,0:T(8,128)(2,1)}, u32[]{:S(2)}) copy-start(bf16[4,128,640]{1,2,0:T(8,128)(2,1)} %fusion.5) | copy-start | bytes 1966084
  148.6 14.1 %collective-permute-start.10 = (bf16[2,128,512]{2,1,0:T(8,128)(2,1)S(1)}, bf16[2,128,512]{2,1,0:T(8,128)(2,1)S(1)}, u32[]{:S(2)}, u32[]{:S(2)}) collective-permute-start(bf16[2,128,512]{2,1,0:T(8,128)(2,1)S(1)} %get-tuple-element.20), channel_id=1, source_target_pairs={{4,0},{8,4},{12,8},{16,12},{20,16},{24,20},{28,24},{32,28},{36,32}... | collective-permute-start | bytes 786440 | tf_op jit(solution)/shard_map/ppermute | solution.py:15
  163.7 14.3 %collective-permute-start.9 = (bf16[2,128,512]{2,1,0:T(8,128)(2,1)}, bf16[2,128,512]{2,1,0:T(8,128)(2,1)}, u32[]{:S(2)}, u32[]{:S(2)}) collective-permute-start(bf16[2,128,512]{2,1,0:T(8,128)(2,1)} %get-tuple-element.17), channel_id=1, source_target_pairs={{0,4},{4,8},{8,12},{12,16},{16,20},{20,24},{24,28},{28,32},{32,36}... | collective-permute-start | bytes 786440 | tf_op jit(solution)/shard_map/ppermute | solution.py:15
  165.6 13.3 %collective-permute-start.11 = (bf16[2,128,512]{2,1,0:T(8,128)(2,1)}, bf16[2,128,512]{2,1,0:T(8,128)(2,1)}, u32[]{:S(2)}, u32[]{:S(2)}) collective-permute-start(bf16[2,128,512]{2,1,0:T(8,128)(2,1)} %get-tuple-element.18), channel_id=1, source_target_pairs={{4,0},{8,4},{12,8},{16,12},{20,16},{24,20},{28,24},{32,28},{36,32}... | collective-permute-start | bytes 786440 | tf_op jit(solution)/shard_map/ppermute | solution.py:15
Sparse Core Ops, SparseCore 0:
  46.6 45.5 reduce-scatter.1
where the time goes:
time: 190 us; the launch traced here: 188 us
  starting transfers between devices  64 us (34%)
  waiting for transfers between devices  61.3 us (32%)
  between operations  14.7 us (8%)
  local copies, waits for them, and re-layouts  14.6 us (8%)
  blocking collectives  13.8 us (7%)
  other arithmetic  9.99 us (5%)
  matrix products  9.27 us (5%)
    ppermute x8, starting transfers between devices, shifted(): return lax.ppermute(block, axis, route)  44.9 us
    reduce_scatter x1, waiting for transfers between devices, per_device(): lax.psum_scatter(partial_out.astype(jnp.bfloat16), 'mp', scatter_dimensio...  43.9 us
    ppermute x8, waiting for transfers between devices, shifted(): return lax.ppermute(block, axis, route)  16.5 us
    ppermute x2, starting transfers between devices, with_halo(): lax.ppermute(lax.slice_in_dim(block, 0, width, axis=dim), axis, backward)  13.9 us
    all_gather x1, blocking collectives, per_device(): lax.all_gather(grad_input, 'mp', axis=1, tiled=True)  13.8 us
    ppermute x2, starting transfers between devices, with_halo(): lax.ppermute(lax.slice_in_dim(block, block.shape[dim] - width, None, axis...  5.19 us
    another operation x2, local copies, waits for them, and re-layouts, per_device(): jnp.stack([key_parts.reshape(window_len, local_width), value_parts.reshap...  4.56 us
    unnamed x68, local copies, waits for them, and re-layouts  4.26 us
  transfers between devices with their start and end apart: 13, of which 9 were waited for; matrix products, arithmetic and copies ran while one was open for 3% of the time, Pallas kernels for 0%

commit v1 on v0

v1 whole, which is shorter than its diff:
```python
import functools
import math

import jax
import jax.numpy as jnp
from jax import lax
from jax.experimental import pallas as pl
from jax.experimental.pallas import tpu as pltpu
from jax.sharding import PartitionSpec as P

HDIM = 128
LOOK = 2
BLOCKS = 2 * LOOK + 1
RIM = 32
HALF = 16
MESH = pl.DeviceIdType.MESH
F32 = jnp.float32
BF16 = jnp.bfloat16


def nt(a, b):
    return lax.dot_general(a, b, (((1,), (1,)), ((), ())), preferred_element_type=F32)


def nn(a, b):
    return jnp.dot(a, b, preferred_element_type=F32)


def kernel_body(
    count,
    heads,
    q_hbm,
    k_hbm,
    v_hbm,
    in_hbm,
    w_hbm,
    tap_hbm,
    cot_hbm,
    out_hbm,
    gi_hbm,
    gq_hbm,
    gk_hbm,
    gv_hbm,
    qwin,
    kwin,
    vwin,
    dowin,
    lsewin,
    deltawin,
    probs,
    probs_t,
    att,
    w_own,
    w_sib,
    taps,
    inp,
    cotp,
    own_sum,
    part_send,
    part_recv,
    rim_send,
    rim_own,
    rim_far,
    hpad,
    gpad,
    gfull,
    out_v,
    gq_v,
    gk_v,
    gv_v,
    local_sem,
    out_sem,
    kv_send,
    kv_recv,
    q_send,
    q_recv,
    lse_send,
    lse_recv,
    do_send,
    do_recv,
    delta_send,
    delta_recv,
    w_send,
    w_recv,
    cot_send,
    cot_recv,
    att_send,
    att_recv,
    part_ssem,
    part_rsem,
    rim_ssem,
    rim_rsem,
    gi_send,
    gi_recv,
):
    frames, width = inp.shape
    ntaps = taps.shape[0]
    scale = 1.0 / math.sqrt(HDIM)
    c = lax.axis_index("ctx")
    m = lax.axis_index("mp")
    right = lax.rem(c + 1, count)
    right2 = lax.rem(c + 2, count)
    left = lax.rem(c + count - 1, count)
    left2 = lax.rem(c + count - 2, count)
    sib_m = m + 1 - 2 * lax.rem(m, 2)
    far_m = lax.rem(m + 2, 4)
    far_sib_m = lax.rem(sib_m + 2, 4)
    sib = (c, sib_m)
    far = (c, far_m)

    barrier = pltpu.get_barrier_semaphore()
    partners = [
        (right, m), (left, m), (right2, m), (left2, m),
        sib, far, (right, far_m), (left, far_m),
    ]
    for device in partners:
        pl.semaphore_signal(barrier, inc=1, device_id=device, device_id_type=MESH)

    def local(src, dst, at):
        copy = pltpu.make_async_copy(src, dst, local_sem.at[at])
        copy.start()
        return copy

    def remote(src, dst, send, recv, device):
        return pltpu.make_async_remote_copy(
            src_ref=src, dst_ref=dst, send_sem=send, recv_sem=recv,
            device_id=device, device_id_type=MESH,
        )

    def cols(index):
        return slice(index * HDIM, (index + 1) * HDIM)

    def block(slot):
        return slice(slot * frames, (slot + 1) * frames)

    def wide(index):
        return pl.ds(pl.multiple_of(index * width, width), width)

    mid = block(LOOK)
    loads = {}
    for h in range(heads):
        loads["q", h] = local(q_hbm.at[:, cols(h)], qwin.at[h, mid], h)
        loads["k", h] = local(k_hbm.at[:, cols(h)], kwin.at[h, mid], heads + h)
        loads["v", h] = local(v_hbm.at[:, cols(h)], vwin.at[h, mid], 2 * heads + h)
    at = 3 * heads
    loads["w"] = local(w_hbm, w_own, at)
    loads["taps"] = local(tap_hbm, taps, at + 1)
    loads["inp"] = local(in_hbm, inp, at + 2)
    loads["cot"] = local(cot_hbm, cotp.at[HALF : HALF + frames], at + 3)

    pl.semaphore_wait(barrier, len(partners))

    first = {}
    second = {}
    for h in range(heads):
        for i, (src, win) in enumerate(((k_hbm, kwin), (v_hbm, vwin))):
            first[h, i, 0] = remote(
                src.at[:, cols(h)], win.at[h, block(1)], kv_send.at[0, i, h], kv_recv.at[0, i, h], (right, m)
            )
            first[h, i, 1] = remote(
                src.at[:, cols(h)], win.at[h, block(3)], kv_send.at[1, i, h], kv_recv.at[1, i, h], (left, m)
            )
            first[h, i, 0].start()
            first[h, i, 1].start()
            second[h, i, 0] = remote(
                win.at[h, block(1)], win.at[h, block(0)], kv_send.at[2, i, h], kv_recv.at[2, i, h], (right, m)
            )
            second[h, i, 1] = remote(
                win.at[h, block(3)], win.at[h, block(4)], kv_send.at[3, i, h], kv_recv.at[3, i, h], (left, m)
            )

    early = [
        remote(w_hbm.at[:, wide(sib_m)], w_sib.at[0], w_send.at[0], w_recv.at[0], sib),
        remote(w_hbm.at[:, wide(far_sib_m)], w_sib.at[1], w_send.at[1], w_recv.at[1], sib),
        remote(
            cot_hbm.at[frames - HALF : frames], cotp.at[0:HALF], cot_send.at[0], cot_recv.at[0], (right, m)
        ),
        remote(
            cot_hbm.at[0:HALF],
            cotp.at[HALF + frames : 2 * HALF + frames],
            cot_send.at[1],
            cot_recv.at[1],
            (left, m),
        ),
    ]
    for copy in early:
        copy.start()

    for h in range(heads):
        for side in range(2):
            for i in range(2):
                first[h, i, side].wait_recv()
                second[h, i, side].start()

    owner = lax.shift_right_logical(
        lax.broadcasted_iota(jnp.int32, (1, BLOCKS * frames), 1), 7
    ) + c
    valid = (owner >= LOOK) & (owner < count + LOOK)
    lane = lax.broadcasted_iota(jnp.int32, (frames, HDIM), 1)

    stat = jnp.zeros((frames, HDIM), F32)
    shares = []
    for h in range(heads):
        loads["q", h].wait()
        loads["k", h].wait()
        loads["v", h].wait()
        for side in range(2):
            for i in range(2):
                second[h, i, side].wait_recv()
        scores = nt(qwin[h, mid], kwin[h]) * scale
        scores = jnp.where(valid, scores, -jnp.inf)
        top = jnp.max(scores, axis=1, keepdims=True)
        weights = jnp.exp(scores - top)
        total = jnp.sum(weights, axis=1, keepdims=True)
        stat = jnp.where(lane == h, top + jnp.log(total), stat)
        prob = weights * (1.0 / total)
        probs[h] = prob
        att[0, :, cols(h)] = nn(prob.astype(BF16), vwin[h]).astype(BF16)
        share = remote(att.at[0, :, cols(h)], att.at[1, :, cols(h)], att_send.at[h], att_recv.at[h], sib)
        share.start()
        shares.append(share)
    lsewin[:, mid] = jnp.transpose(stat)[0:8]

    loads["w"].wait()
    far_part = nn(att[0], w_own[:, wide(far_m)])
    own_part = nn(att[0], w_own[:, wide(m)])
    early[0].wait_recv()
    early[1].wait_recv()
    for share in shares:
        share.wait_recv()
    part_send[...] = (far_part + nn(att[1], w_sib[1])).astype(BF16)
    parts = [
        remote(part_send, part_recv, part_ssem, part_rsem, far),
        remote(
            part_send.at[frames - RIM : frames], rim_far.at[0], rim_ssem.at[0], rim_rsem.at[0], (right, far_m)
        ),
        remote(part_send.at[0:RIM], rim_far.at[1], rim_ssem.at[1], rim_rsem.at[1], (left, far_m)),
    ]
    for copy in parts:
        copy.start()
    loads["inp"].wait()
    summed = own_part + nn(att[1], w_sib[0]) + inp[...].astype(F32)
    own_sum[...] = summed
    rim_send[0] = summed[frames - RIM : frames].astype(BF16)
    rim_send[1] = summed[0:RIM].astype(BF16)
    rims = [
        remote(rim_send.at[0], rim_own.at[0], rim_ssem.at[2], rim_rsem.at[2], (right, m)),
        remote(rim_send.at[1], rim_own.at[1], rim_ssem.at[3], rim_rsem.at[3], (left, m)),
    ]
    for copy in rims:
        copy.start()

    routes = [((right, m), 1), ((left, m), 3), ((right2, m), 0), ((left2, m), 4)]
    queries = []
    for i, (device, slot) in enumerate(routes):
        queries.append(
            remote(qwin.at[:, mid], qwin.at[:, block(slot)], q_send.at[i], q_recv.at[i], device)
        )
        queries.append(
            remote(lsewin.at[:, mid], lsewin.at[:, block(slot)], lse_send.at[i], lse_recv.at[i], device)
        )
    for copy in queries:
        copy.start()

    loads["taps"].wait()
    loads["cot"].wait()
    early[2].wait_recv()
    early[3].wait_recv()
    for copy in parts + rims:
        copy.wait_recv()

    row = lax.broadcasted_iota(jnp.int32, (frames + 2 * HALF, HDIM), 0)
    inside = ((row >= HALF) | (c > 0)) & ((row < HALF + frames) | (c < count - 1))
    spread = []
    for j in range(width // HDIM):
        lanes = cols(j)
        hidden = (own_sum[:, lanes] + part_recv[:, lanes].astype(F32)).astype(BF16).astype(F32)
        hpad[j, RIM : RIM + frames] = hidden
        low = (rim_own[0, :, lanes].astype(F32) + rim_far[0, :, lanes].astype(F32)).astype(BF16).astype(F32)
        high = (rim_own[1, :, lanes].astype(F32) + rim_far[1, :, lanes].astype(F32)).astype(BF16).astype(F32)
        hpad[j, 0:RIM] = jnp.where(c > 0, low, 0.0)
        hpad[j, RIM + frames : 2 * RIM + frames] = jnp.where(c < count - 1, high, 0.0)
        conv = jnp.zeros((frames + 2 * HALF, HDIM), F32)
        for tap in range(ntaps):
            conv = conv + taps[tap : tap + 1, lanes] * hpad[j, tap + 1 : tap + 1 + frames + 2 * HALF]
        gate = jax.nn.sigmoid(conv)
        swish = conv * gate
        out_v[:, lanes] = (hidden + swish[HALF : HALF + frames]).astype(BF16)
        cot = cotp[:, lanes].astype(F32)
        grad_conv = (cot * (gate + swish * (1.0 - gate))).astype(BF16).astype(F32)
        gpad[j] = jnp.where(inside, grad_conv, 0.0)
        grad = cot[HALF : HALF + frames]
        for tap in range(ntaps):
            start = 2 * HALF - 1 - tap
            grad = grad + taps[tap : tap + 1, lanes] * gpad[j, start : start + frames]
        gfull[0, :, lanes] = grad.astype(BF16)
        to_sib = remote(gfull.at[0, :, lanes], gfull.at[1, :, lanes], gi_send.at[0, j], gi_recv.at[0, j], sib)
        to_far = remote(gfull.at[0, :, lanes], gfull.at[2, :, lanes], gi_send.at[1, j], gi_recv.at[1, j], far)
        relay = remote(gfull.at[2, :, lanes], gfull.at[3, :, lanes], gi_send.at[2, j], gi_recv.at[2, j], sib)
        to_far.start()
        to_sib.start()
        spread.append((to_sib, to_far, relay))

    stores = [
        pltpu.make_async_copy(out_v, out_hbm, out_sem.at[0]),
        pltpu.make_async_copy(gfull.at[0], gi_hbm, out_sem.at[1]),
    ]
    for copy in stores:
        copy.start()

    for copy in queries:
        copy.wait_recv()
    for h in range(heads):
        scores_t = nt(kwin[h, mid], qwin[h]) * scale
        probs_t[h] = jnp.where(valid, jnp.exp(scores_t - lsewin[h : h + 1]), 0.0)

    up = nt(gfull[0], w_own[:, wide(m)])
    for to_sib, to_far, relay in spread:
        to_far.wait_recv()
        relay.start()
    for to_sib, to_far, relay in spread:
        to_sib.wait_recv()
    up = up + nt(gfull[1], w_own[:, wide(sib_m)])
    up = up + nt(gfull[2], w_own[:, wide(far_m)])
    for to_sib, to_far, relay in spread:
        relay.wait_recv()
    up = up + nt(gfull[3], w_own[:, wide(far_sib_m)])
    upstream = up.astype(BF16)

    delta = []
    stat = jnp.zeros((frames, HDIM), F32)
    for h in range(heads):
        part = upstream[:, cols(h)]
        dowin[h, mid] = part
        delta.append(
            jnp.sum(part.astype(F32) * att[0, :, cols(h)].astype(F32), axis=1, keepdims=True)
        )
        stat = jnp.where(lane == h, delta[h], stat)
    deltawin[:, mid] = jnp.transpose(stat)[0:8]
    ups = []
    for i, (device, slot) in enumerate(routes):
        ups.append(
            remote(dowin.at[:, mid], dowin.at[:, block(slot)], do_send.at[i], do_recv.at[i], device)
        )
        ups.append(
            remote(deltawin.at[:, mid], deltawin.at[:, block(slot)], delta_send.at[i], delta_recv.at[i], device)
        )
    for copy in ups:
        copy.start()

    for h in range(heads):
        dots = nt(dowin[h, mid], vwin[h])
        grad_scores = (probs[h] * (dots - delta[h]) * scale).astype(BF16)
        gq_v[:, cols(h)] = nn(grad_scores, kwin[h]).astype(BF16)
    stores.append(pltpu.make_async_copy(gq_v, gq_hbm, out_sem.at[2]))
    stores[-1].start()

    for copy in ups:
        copy.wait_recv()
    for h in range(heads):
        prob_t = probs_t[h]
        gv_v[:, cols(h)] = nn(prob_t.astype(BF16), dowin[h]).astype(BF16)
        dots_t = nt(vwin[h, mid], dowin[h])
        grad_t = (prob_t * (dots_t - deltawin[h : h + 1]) * scale).astype(BF16)
        gk_v[:, cols(h)] = nn(grad_t, qwin[h]).astype(BF16)
    stores.append(pltpu.make_async_copy(gk_v, gk_hbm, out_sem.at[3]))
    stores[-1].start()
    stores.append(pltpu.make_async_copy(gv_v, gv_hbm, out_sem.at[4]))
    stores[-1].start()

    for copy in list(first.values()) + list(second.values()) + early + shares + parts + rims + queries + ups:
        copy.wait_send()
    for group in spread:
        for copy in group:
            copy.wait_send()
    for copy in stores:
        copy.wait()


def per_device(query_rows, key_rows, value_rows, inputs, out_weight, kernel, cotangent):
    frames, width = query_rows.shape
    heads = width // HDIM
    count = lax.axis_size("ctx")
    window = BLOCKS * frames
    full = out_weight.shape[1]
    chunks = width // HDIM
    taps = kernel.shape[0]
    dma = pltpu.SemaphoreType.DMA
    win = pltpu.VMEM((heads, window, HDIM), BF16)
    scratch = [
        win, win, win, win,
        pltpu.VMEM((8, window), F32),
        pltpu.VMEM((8, window), F32),
        pltpu.VMEM((heads, frames, window), F32),
        pltpu.VMEM((heads, frames, window), F32),
        pltpu.VMEM((2, frames, width), BF16),
        pltpu.VMEM((width, full), BF16),
        pltpu.VMEM((2, width, width), BF16),
        pltpu.VMEM((taps, width), F32),
        pltpu.VMEM((frames, width), BF16),
        pltpu.VMEM((frames + 2 * HALF, width), BF16),
        pltpu.VMEM((frames, width), F32),
        pltpu.VMEM((frames, width), BF16),
        pltpu.VMEM((frames, width), BF16),
        pltpu.VMEM((2, RIM, width), BF16),
        pltpu.VMEM((2, RIM, width), BF16),
        pltpu.VMEM((2, RIM, width), BF16),
        pltpu.VMEM((chunks, frames + 2 * RIM, HDIM), F32),
        pltpu.VMEM((chunks, frames + 2 * HALF, HDIM), F32),
        pltpu.VMEM((4, frames, width), BF16),
        pltpu.VMEM((frames, width), BF16),
        pltpu.VMEM((frames, width), BF16),
        pltpu.VMEM((frames, width), BF16),
        pltpu.VMEM((frames, width), BF16),
        dma((3 * heads + 4,)),
        dma((5,)),
        dma((4, 2, heads)), dma((4, 2, heads)),
        dma((4,)), dma((4,)),
        dma((4,)), dma((4,)),
        dma((4,)), dma((4,)),
        dma((4,)), dma((4,)),
        dma((2,)), dma((2,)),
        dma((2,)), dma((2,)),
        dma((heads,)), dma((heads,)),
        dma, dma,
        dma((4,)), dma((4,)),
        dma((3, chunks)), dma((3, chunks)),
    ]
    shape = jax.ShapeDtypeStruct((frames, width), BF16)
    return pl.pallas_call(
        functools.partial(kernel_body, count, heads),
        out_shape=(shape,) * 5,
        in_specs=[pl.BlockSpec(memory_space=pl.ANY)] * 7,
        out_specs=(pl.BlockSpec(memory_space=pl.ANY),) * 5,
        scratch_shapes=scratch,
        compiler_params=pltpu.CompilerParams(
            collective_id=0, has_side_effects=True, vmem_limit_bytes=56 * 1024 * 1024
        ),
        name="conformer",
    )(query_rows, key_rows, value_rows, inputs, out_weight, kernel, cotangent)


def solution(mesh):
    placed = (
        P("ctx", "mp"),
        P("ctx", "mp"),
        P("ctx", "mp"),
        P("ctx", "mp"),
        P("mp", None),
        P(None, "mp"),
        P("ctx", "mp"),
    )
    return jax.shard_map(
        per_device,
        mesh=mesh,
        in_specs=placed,
        out_specs=(P("ctx", "mp"),) * 5,
        check_vma=False,
    )
```

time: 190 us -> 81.8 us (0.43)
  the two profiles are of different devices: /device:TPU:9 before, /device:TPU:72 now
where the time goes in v1:
time: 81.8 us; the launch traced here: 81.6 us
  Pallas kernels  73.1 us (89%)
  local copies, waits for them, and re-layouts  7.84 us (10%)
    pallas_call x1, Pallas kernels, per_device(): pl.pallas_call(functools.partial(kernel_body, count, heads), out_shape=(s...  73.1 us
    unnamed x5, local copies, waits for them, and re-layouts  7.84 us

profile of v1, /device:TPU:72, one launch (start us, length us, event | category | flops | bytes accessed | tf_op | source)
XLA Modules:
  0.0 81.6 jit_solution(1761415969030582877)
XLA Ops:
  0.6 73.1 %conformer.1 = (bf16[128,512]{1,0:T(8,128)(2,1)}, bf16[128,512]{1,0:T(8,128)(2,1)}, bf16[128,512]{1,0:T(8,128)(2,1)}, bf16[128,512]{1,0:T(8,128)(2,1)}, bf16[128,512]{1,0:T(8,128)(2,1)}) custom-call(bf16[128,512]{1,0:T(8,128)(2,1)} %q_hbm.1, bf16[128,512]{1,0:T(8,128)(2,1)} %k_hbm.1, bf16[128,512]{1,0:T(8,128)(2,1)} %v_hbm.1, bf16[128,512]{1,0:T(8,128)(2,1)} %in_hbm.1, ...), custom_call_target="tpu_custom_call" | custom-call | tf_op jit(solution)/shard_map/conformer/pallas_call | solution.py:430
  73.7 1.6 %copy.17 = bf16[128,512]{1,0:T(8,128)(2,1)} copy(bf16[128,512]{1,0:T(8,128)(2,1)} %get-tuple-element.10) | data formatting | bytes 262144
  75.3 1.6 %copy.18 = bf16[128,512]{1,0:T(8,128)(2,1)} copy(bf16[128,512]{1,0:T(8,128)(2,1)} %get-tuple-element.11) | data formatting | bytes 262144
  76.9 1.6 %copy.19 = bf16[128,512]{1,0:T(8,128)(2,1)} copy(bf16[128,512]{1,0:T(8,128)(2,1)} %get-tuple-element.12) | data formatting | bytes 262144
  78.4 1.6 %copy.20 = bf16[128,512]{1,0:T(8,128)(2,1)} copy(bf16[128,512]{1,0:T(8,128)(2,1)} %get-tuple-element.13) | data formatting | bytes 262144
  80.0 1.6 %copy.21 = bf16[128,512]{1,0:T(8,128)(2,1)} copy(bf16[128,512]{1,0:T(8,128)(2,1)} %get-tuple-element.14) | data formatting | bytes 262144

commit v2 on v1

--- a/solution.py
+++ b/solution.py
@@ -68,6 +68,8 @@
     gq_v,
     gk_v,
     gv_v,
+    gk_sum,
+    gv_sum,
     local_sem,
     out_sem,
     kv_send,
@@ -109,10 +111,22 @@
     far = (c, far_m)
 
     barrier = pltpu.get_barrier_semaphore()
-    partners = [
-        (right, m), (left, m), (right2, m), (left2, m),
-        sib, far, (right, far_m), (left, far_m),
-    ]
+    exists = [c < count - 1, c > 0, c < count - 2, c > 1]
+    targets = [right, left, right2, left2]
+    places = [1, 3, 0, 4]
+
+    def toward(i, plane=None):
+        other = sib_m if plane is None else plane
+        own = m if plane is None else plane
+        return (jnp.where(exists[i], targets[i], c), jnp.where(exists[i], own, other))
+
+    def turned(i, value, mirrored):
+        return jnp.where(exists[i], value, mirrored)
+
+    def place(i, slot):
+        return pl.ds(pl.multiple_of(turned(i, slot, 4 - slot) * frames, frames), frames)
+
+    partners = [toward(i) for i in range(4)] + [sib, far, toward(0, far_m), toward(1, far_m)]
     for device in partners:
         pl.semaphore_signal(barrier, inc=1, device_id=device, device_id_type=MESH)
 
@@ -125,6 +139,15 @@
         return pltpu.make_async_remote_copy(
             src_ref=src, dst_ref=dst, send_sem=send, recv_sem=recv,
             device_id=device, device_id_type=MESH,
+        )
+
+    class Crossing:
+        def __init__(self, sent, due):
+            self.start, self.wait_send, self.wait_recv = sent.start, sent.wait_send, due.wait_recv
+
+    def shift(src, dst, due_dst, send, recv, due_recv, device):
+        return Crossing(
+            remote(src, dst, send, recv, device), remote(src, due_dst, send, due_recv, device)
         )
 
     def cols(index):
@@ -154,35 +177,32 @@
     second = {}
     for h in range(heads):
         for i, (src, win) in enumerate(((k_hbm, kwin), (v_hbm, vwin))):
-            first[h, i, 0] = remote(
-                src.at[:, cols(h)], win.at[h, block(1)], kv_send.at[0, i, h], kv_recv.at[0, i, h], (right, m)
-            )
-            first[h, i, 1] = remote(
-                src.at[:, cols(h)], win.at[h, block(3)], kv_send.at[1, i, h], kv_recv.at[1, i, h], (left, m)
-            )
-            first[h, i, 0].start()
-            first[h, i, 1].start()
-            second[h, i, 0] = remote(
-                win.at[h, block(1)], win.at[h, block(0)], kv_send.at[2, i, h], kv_recv.at[2, i, h], (right, m)
-            )
-            second[h, i, 1] = remote(
-                win.at[h, block(3)], win.at[h, block(4)], kv_send.at[3, i, h], kv_recv.at[3, i, h], (left, m)
-            )
+            for side in range(2):
+                near_slot, far_slot = places[side], places[2 + side]
+                first[h, i, side] = shift(
+                    src.at[:, cols(h)], win.at[h, place(side, near_slot)], win.at[h, block(near_slot)],
+                    kv_send.at[side, i, h], kv_recv.at[turned(side, side, 1 - side), i, h],
+                    kv_recv.at[side, i, h], toward(side),
+                )
+                first[h, i, side].start()
+                second[h, i, side] = shift(
+                    win.at[h, block(near_slot)], win.at[h, place(side, far_slot)], win.at[h, block(far_slot)],
+                    kv_send.at[2 + side, i, h], kv_recv.at[2 + turned(side, side, 1 - side), i, h],
+                    kv_recv.at[2 + side, i, h], toward(side),
+                )
 
     early = [
         remote(w_hbm.at[:, wide(sib_m)], w_sib.at[0], w_send.at[0], w_recv.at[0], sib),
         remote(w_hbm.at[:, wide(far_sib_m)], w_sib.at[1], w_send.at[1], w_recv.at[1], sib),
-        remote(
-            cot_hbm.at[frames - HALF : frames], cotp.at[0:HALF], cot_send.at[0], cot_recv.at[0], (right, m)
-        ),
-        remote(
-            cot_hbm.at[0:HALF],
-            cotp.at[HALF + frames : 2 * HALF + frames],
-            cot_send.at[1],
-            cot_recv.at[1],
-            (left, m),
-        ),
     ]
+    cot_starts = (0, HALF + frames)
+    for side, rows in enumerate((slice(frames - HALF, frames), slice(0, HALF))):
+        start = turned(side, cot_starts[side], cot_starts[1 - side])
+        early.append(shift(
+            cot_hbm.at[rows], cotp.at[pl.ds(pl.multiple_of(start, HALF), HALF)],
+            cotp.at[cot_starts[side] : cot_starts[side] + HALF],
+            cot_send.at[side], cot_recv.at[turned(side, side, 1 - side)], cot_recv.at[side], toward(side),
+        ))
     for copy in early:
         copy.start()
 
@@ -197,6 +217,22 @@
     ) + c
     valid = (owner >= LOOK) & (owner < count + LOOK)
     lane = lax.broadcasted_iota(jnp.int32, (frames, HDIM), 1)
+
+    def spread_to(i, win, send, recv, source=mid):
+        return shift(
+            win.at[:, source], win.at[:, place(i, places[i])], win.at[:, block(places[i])],
+            send.at[i], recv.at[turned(i, i, i ^ 1)], recv.at[i], toward(i),
+        )
+
+    def relay_to(side, win, send, recv):
+        near_slot, far_slot = places[side], places[2 + side]
+        return shift(
+            win.at[:, block(near_slot)], win.at[:, place(side, far_slot)], win.at[:, block(far_slot)],
+            send.at[2 + side], recv.at[2 + turned(side, side, 1 - side)], recv.at[2 + side], toward(side),
+        )
+
+    queries = [spread_to(side, qwin, q_send, q_recv) for side in range(2)]
+    queries += [relay_to(side, qwin, q_send, q_recv) for side in range(2)]
 
     stat = jnp.zeros((frames, HDIM), F32)
     shares = []
@@ -207,6 +243,9 @@
         for side in range(2):
             for i in range(2):
                 second[h, i, side].wait_recv()
+        if h == heads - 1:
+            queries[0].start()
+            queries[1].start()
         scores = nt(qwin[h, mid], kwin[h]) * scale
         scores = jnp.where(valid, scores, -jnp.inf)
         top = jnp.max(scores, axis=1, keepdims=True)
@@ -222,60 +261,77 @@
     lsewin[:, mid] = jnp.transpose(stat)[0:8]
 
     loads["w"].wait()
-    far_part = nn(att[0], w_own[:, wide(far_m)])
-    own_part = nn(att[0], w_own[:, wide(m)])
     early[0].wait_recv()
     early[1].wait_recv()
     for share in shares:
         share.wait_recv()
-    part_send[...] = (far_part + nn(att[1], w_sib[1])).astype(BF16)
-    parts = [
-        remote(part_send, part_recv, part_ssem, part_rsem, far),
-        remote(
-            part_send.at[frames - RIM : frames], rim_far.at[0], rim_ssem.at[0], rim_rsem.at[0], (right, far_m)
-        ),
-        remote(part_send.at[0:RIM], rim_far.at[1], rim_ssem.at[1], rim_rsem.at[1], (left, far_m)),
-    ]
-    for copy in parts:
-        copy.start()
+    parts = []
+    for j in range(width // HDIM):
+        lanes = cols(j)
+        far_cols = pl.ds(pl.multiple_of(far_m * width + j * HDIM, HDIM), HDIM)
+        part_send[:, lanes] = (nn(att[0], w_own[:, far_cols]) + nn(att[1], w_sib[1, :, lanes])).astype(BF16)
+        group = [
+            remote(part_send.at[:, lanes], part_recv.at[:, lanes], part_ssem.at[j], part_rsem.at[j], far)
+        ]
+        for side, rows in enumerate((slice(frames - RIM, frames), slice(0, RIM))):
+            turn = turned(side, side, 1 - side)
+            group.append(shift(
+                part_send.at[rows, lanes], rim_far.at[turn, :, lanes], rim_far.at[side, :, lanes],
+                rim_ssem.at[side, j], rim_rsem.at[turn, j], rim_rsem.at[side, j], toward(side, far_m),
+            ))
+        for copy in group:
+            copy.start()
+        parts.append(group)
     loads["inp"].wait()
+    own_part = nn(att[0], w_own[:, wide(m)])
     summed = own_part + nn(att[1], w_sib[0]) + inp[...].astype(F32)
     own_sum[...] = summed
+
+    rims = []
     rim_send[0] = summed[frames - RIM : frames].astype(BF16)
     rim_send[1] = summed[0:RIM].astype(BF16)
-    rims = [
-        remote(rim_send.at[0], rim_own.at[0], rim_ssem.at[2], rim_rsem.at[2], (right, m)),
-        remote(rim_send.at[1], rim_own.at[1], rim_ssem.at[3], rim_rsem.at[3], (left, m)),
-    ]
-    for copy in rims:
-        copy.start()
-
-    routes = [((right, m), 1), ((left, m), 3), ((right2, m), 0), ((left2, m), 4)]
-    queries = []
-    for i, (device, slot) in enumerate(routes):
-        queries.append(
-            remote(qwin.at[:, mid], qwin.at[:, block(slot)], q_send.at[i], q_recv.at[i], device)
-        )
-        queries.append(
-            remote(lsewin.at[:, mid], lsewin.at[:, block(slot)], lse_send.at[i], lse_recv.at[i], device)
-        )
-    for copy in queries:
+    for j in range(width // HDIM):
+        lanes = cols(j)
+        pair = []
+        for side in range(2):
+            turn = turned(side, side, 1 - side)
+            pair.append(shift(
+                rim_send.at[side, :, lanes], rim_own.at[turn, :, lanes], rim_own.at[side, :, lanes],
+                rim_ssem.at[2 + side, j], rim_rsem.at[2 + turn, j], rim_rsem.at[2 + side, j], toward(side),
+            ))
+            pair[-1].start()
+        rims.append(pair)
+
+    for side in range(2):
+        queries[side].wait_recv()
+        queries[2 + side].start()
+    totals = [spread_to(i, lsewin, lse_send, lse_recv) for i in range(4)]
+    for copy in totals:
         copy.start()
 
     loads["taps"].wait()
     loads["cot"].wait()
     early[2].wait_recv()
     early[3].wait_recv()
-    for copy in parts + rims:
-        copy.wait_recv()
 
     row = lax.broadcasted_iota(jnp.int32, (frames + 2 * HALF, HDIM), 0)
     inside = ((row >= HALF) | (c > 0)) & ((row < HALF + frames) | (c < count - 1))
     spread = []
+
+    def take(j):
+        lanes = cols(j)
+        for copy in parts[j]:
+            copy.wait_recv()
+        hidden = (own_sum[:, lanes] + part_recv[:, lanes].astype(F32)).astype(BF16)
+        hpad[j, RIM : RIM + frames] = hidden.astype(F32)
+
+    take(0)
     for j in range(width // HDIM):
+        if j + 1 < width // HDIM:
+            take(j + 1)
         lanes = cols(j)
-        hidden = (own_sum[:, lanes] + part_recv[:, lanes].astype(F32)).astype(BF16).astype(F32)
-        hpad[j, RIM : RIM + frames] = hidden
+        for copy in rims[j]:
+            copy.wait_recv()
         low = (rim_own[0, :, lanes].astype(F32) + rim_far[0, :, lanes].astype(F32)).astype(BF16).astype(F32)
         high = (rim_own[1, :, lanes].astype(F32) + rim_far[1, :, lanes].astype(F32)).astype(BF16).astype(F32)
         hpad[j, 0:RIM] = jnp.where(c > 0, low, 0.0)
@@ -285,7 +341,7 @@
             conv = conv + taps[tap : tap + 1, lanes] * hpad[j, tap + 1 : tap + 1 + frames + 2 * HALF]
         gate = jax.nn.sigmoid(conv)
         swish = conv * gate
-        out_v[:, lanes] = (hidden + swish[HALF : HALF + frames]).astype(BF16)
+        out_v[:, lanes] = (hpad[j, RIM : RIM + frames] + swish[HALF : HALF + frames]).astype(BF16)
         cot = cotp[:, lanes].astype(F32)
         grad_conv = (cot * (gate + swish * (1.0 - gate))).astype(BF16).astype(F32)
         gpad[j] = jnp.where(inside, grad_conv, 0.0)
@@ -308,7 +364,7 @@
     for copy in stores:
         copy.start()
 
-    for copy in queries:
+    for copy in queries[2:] + totals:
         copy.wait_recv()
     for h in range(heads):
         scores_t = nt(kwin[h, mid], qwin[h]) * scale
@@ -338,42 +394,81 @@
         stat = jnp.where(lane == h, delta[h], stat)
     deltawin[:, mid] = jnp.transpose(stat)[0:8]
     ups = []
-    for i, (device, slot) in enumerate(routes):
-        ups.append(
-            remote(dowin.at[:, mid], dowin.at[:, block(slot)], do_send.at[i], do_recv.at[i], device)
-        )
-        ups.append(
-            remote(deltawin.at[:, mid], deltawin.at[:, block(slot)], delta_send.at[i], delta_recv.at[i], device)
-        )
-    for copy in ups:
+    second_ups = []
+    for h in range(heads):
+        for side in range(2):
+            turn = turned(side, side, 1 - side)
+            near_slot, far_slot = places[side], places[2 + side]
+            ups.append(shift(
+                dowin.at[h, mid], dowin.at[h, place(side, near_slot)], dowin.at[h, block(near_slot)],
+                do_send.at[side, h], do_recv.at[turn, h], do_recv.at[side, h], toward(side),
+            ))
+            ups[-1].start()
+            second_ups.append(shift(
+                dowin.at[h, block(near_slot)], dowin.at[h, place(side, far_slot)], dowin.at[h, block(far_slot)],
+                do_send.at[2 + side, h], do_recv.at[2 + turn, h], do_recv.at[2 + side, h], toward(side),
+            ))
+    deltas = [spread_to(i, deltawin, delta_send, delta_recv) for i in range(4)]
+    for copy in deltas:
         copy.start()
 
-    for h in range(heads):
+    def query_grad(h):
         dots = nt(dowin[h, mid], vwin[h])
         grad_scores = (probs[h] * (dots - delta[h]) * scale).astype(BF16)
         gq_v[:, cols(h)] = nn(grad_scores, kwin[h]).astype(BF16)
+
+    def key_grad(h, span):
+        prob_t = probs_t[h, :, span]
+        d_value = nn(prob_t.astype(BF16), dowin[h, span])
+        dots_t = nt(vwin[h, mid], dowin[h, span])
+        grad_t = (prob_t * (dots_t - deltawin[h : h + 1, span]) * scale).astype(BF16)
+        return nn(grad_t, qwin[h, span]), d_value
+
+    for h in range(heads):
+        query_grad(h)
     stores.append(pltpu.make_async_copy(gq_v, gq_hbm, out_sem.at[2]))
     stores[-1].start()
-
-    for copy in ups:
+    for one, two in zip(ups, second_ups):
+        one.wait_recv()
+        two.start()
+    for copy in deltas:
         copy.wait_recv()
-    for h in range(heads):
-        prob_t = probs_t[h]
-        gv_v[:, cols(h)] = nn(prob_t.astype(BF16), dowin[h]).astype(BF16)
-        dots_t = nt(vwin[h, mid], dowin[h])
-        grad_t = (prob_t * (dots_t - deltawin[h : h + 1]) * scale).astype(BF16)
-        gk_v[:, cols(h)] = nn(grad_t, qwin[h]).astype(BF16)
+    near = slice(frames, 4 * frames)
+    for h in range(heads):
+        gk_sum[:, cols(h)], gv_sum[:, cols(h)] = key_grad(h, near)
+    for h in range(heads):
+        for side in range(2):
+            second_ups[2 * h + side].wait_recv()
+        low_k, low_v = key_grad(h, block(0))
+        high_k, high_v = key_grad(h, block(4))
+        gk_v[:, cols(h)] = (gk_sum[:, cols(h)] + low_k + high_k).astype(BF16)
+        gv_v[:, cols(h)] = (gv_sum[:, cols(h)] + low_v + high_v).astype(BF16)
     stores.append(pltpu.make_async_copy(gk_v, gk_hbm, out_sem.at[3]))
     stores[-1].start()
     stores.append(pltpu.make_async_copy(gv_v, gv_hbm, out_sem.at[4]))
     stores[-1].start()
 
-    for copy in list(first.values()) + list(second.values()) + early + shares + parts + rims + queries + ups:
+    for copy in list(first.values()) + list(second.values()) + early + shares + queries + totals:
         copy.wait_send()
-    for group in spread:
+    for copy in ups + second_ups + deltas:
+        copy.wait_send()
+    for group in parts + rims + spread:
         for copy in group:
             copy.wait_send()
     for copy in stores:
+        copy.wait()
+
+
+def copy_out(*refs):
+    sources, targets, held, sems = refs[:5], refs[5:10], refs[10], refs[11]
+    taken = [pltpu.make_async_copy(source, held.at[i], sems.at[0, i]) for i, source in enumerate(sources)]
+    given = [pltpu.make_async_copy(held.at[i], target, sems.at[1, i]) for i, target in enumerate(targets)]
+    for copy in taken:
+        copy.start()
+    for one, two in zip(taken, given):
+        one.wait()
+        two.start()
+    for copy in given:
         copy.wait()
 
 
@@ -412,22 +507,24 @@
         pltpu.VMEM((frames, width), BF16),
         pltpu.VMEM((frames, width), BF16),
         pltpu.VMEM((frames, width), BF16),
+        pltpu.VMEM((frames, width), F32),
+        pltpu.VMEM((frames, width), F32),
         dma((3 * heads + 4,)),
         dma((5,)),
         dma((4, 2, heads)), dma((4, 2, heads)),
         dma((4,)), dma((4,)),
         dma((4,)), dma((4,)),
-        dma((4,)), dma((4,)),
+        dma((4, heads)), dma((4, heads)),
         dma((4,)), dma((4,)),
         dma((2,)), dma((2,)),
         dma((2,)), dma((2,)),
         dma((heads,)), dma((heads,)),
-        dma, dma,
-        dma((4,)), dma((4,)),
+        dma((chunks,)), dma((chunks,)),
+        dma((4, chunks)), dma((4, chunks)),
         dma((3, chunks)), dma((3, chunks)),
     ]
     shape = jax.ShapeDtypeStruct((frames, width), BF16)
-    return pl.pallas_call(
+    results = pl.pallas_call(
         functools.partial(kernel_body, count, heads),
         out_shape=(shape,) * 5,
         in_specs=[pl.BlockSpec(memory_space=pl.ANY)] * 7,
@@ -438,6 +535,15 @@
         ),
         name="conformer",
     )(query_rows, key_rows, value_rows, inputs, out_weight, kernel, cotangent)
+    return pl.pallas_call(
+        copy_out,
+        out_shape=(shape,) * 5,
+        in_specs=[pl.BlockSpec(memory_space=pl.ANY)] * 5,
+        out_specs=(pl.BlockSpec(memory_space=pl.ANY),) * 5,
+        scratch_shapes=[pltpu.VMEM((5, frames, width), BF16), dma((2, 5))],
+        compiler_params=pltpu.CompilerParams(vmem_limit_bytes=56 * 1024 * 1024),
+        name="copy_out",
+    )(*results)
 
 
 def solution(mesh):

time: 81.8 us -> 72.4 us (0.89)
  the two profiles are of different devices: /device:TPU:72 before, /device:TPU:9 now
where the time goes in v2:
time: 72.4 us; the launch traced here: 72.1 us
  Pallas kernels  71.5 us (99%)
    pallas_call x1, Pallas kernels, per_device(): pl.pallas_call(functools.partial(kernel_body, count, heads), out_shape=(s...  69.6 us
    pallas_call x1, Pallas kernels, per_device(): pl.pallas_call(copy_out, out_shape=(shape,) * 5, in_specs=[pl.BlockSpec(m...  1.91 us

profile of v2, /device:TPU:9, one launch (start us, length us, event | category | flops | bytes accessed | tf_op | source)
XLA Modules:
  0.0 72.1 jit_solution(2286855355744472990)
XLA Ops:
  0.6 69.6 %conformer.1 = (bf16[128,512]{1,0:T(8,128)(2,1)}, bf16[128,512]{1,0:T(8,128)(2,1)}, bf16[128,512]{1,0:T(8,128)(2,1)}, bf16[128,512]{1,0:T(8,128)(2,1)}, bf16[128,512]{1,0:T(8,128)(2,1)}) custom-call(bf16[128,512]{1,0:T(8,128)(2,1)} %q_hbm.1, bf16[128,512]{1,0:T(8,128)(2,1)} %k_hbm.1, bf16[128,512]{1,0:T(8,128)(2,1)} %v_hbm.1, bf16[128,512]{1,0:T(8,128)(2,1)} %in_hbm.1, ...), custom_call_target="tpu_custom_call" | custom-call | tf_op jit(solution)/shard_map/conformer/pallas_call | solution.py:527
  70.2 1.9 %copy_out.1 = (bf16[128,512]{1,0:T(8,128)(2,1)}, bf16[128,512]{1,0:T(8,128)(2,1)}, bf16[128,512]{1,0:T(8,128)(2,1)}, bf16[128,512]{1,0:T(8,128)(2,1)}, bf16[128,512]{1,0:T(8,128)(2,1)}) custom-call(bf16[128,512]{1,0:T(8,128)(2,1)} %get-tuple-element.10.refs_0_, bf16[128,512]{1,0:T(8,128)(2,1)} %get-tuple-element.11.refs_1_, ...), custom_call_target="tpu_custom_call" | custom-call | tf_op jit(solution)/shard_map/copy_out/pallas_call | solution.py:538

commit v3 on v2

--- a/solution.py
+++ b/solution.py
@@ -60,7 +60,6 @@
     part_recv,
     rim_send,
     rim_own,
-    rim_far,
     hpad,
     gpad,
     gfull,
@@ -126,7 +125,7 @@
     def place(i, slot):
         return pl.ds(pl.multiple_of(turned(i, slot, 4 - slot) * frames, frames), frames)
 
-    partners = [toward(i) for i in range(4)] + [sib, far, toward(0, far_m), toward(1, far_m)]
+    partners = [toward(i) for i in range(4)] + [sib, far]
     for device in partners:
         pl.semaphore_signal(barrier, inc=1, device_id=device, device_id_type=MESH)
 
@@ -203,14 +202,14 @@
             cotp.at[cot_starts[side] : cot_starts[side] + HALF],
             cot_send.at[side], cot_recv.at[turned(side, side, 1 - side)], cot_recv.at[side], toward(side),
         ))
-    for copy in early:
-        copy.start()
-
     for h in range(heads):
         for side in range(2):
             for i in range(2):
                 first[h, i, side].wait_recv()
                 second[h, i, side].start()
+
+    for copy in early:
+        copy.start()
 
     owner = lax.shift_right_logical(
         lax.broadcasted_iota(jnp.int32, (1, BLOCKS * frames), 1), 7
@@ -273,12 +272,6 @@
         group = [
             remote(part_send.at[:, lanes], part_recv.at[:, lanes], part_ssem.at[j], part_rsem.at[j], far)
         ]
-        for side, rows in enumerate((slice(frames - RIM, frames), slice(0, RIM))):
-            turn = turned(side, side, 1 - side)
-            group.append(shift(
-                part_send.at[rows, lanes], rim_far.at[turn, :, lanes], rim_far.at[side, :, lanes],
-                rim_ssem.at[side, j], rim_rsem.at[turn, j], rim_rsem.at[side, j], toward(side, far_m),
-            ))
         for copy in group:
             copy.start()
         parts.append(group)
@@ -287,24 +280,6 @@
     summed = own_part + nn(att[1], w_sib[0]) + inp[...].astype(F32)
     own_sum[...] = summed
 
-    rims = []
-    rim_send[0] = summed[frames - RIM : frames].astype(BF16)
-    rim_send[1] = summed[0:RIM].astype(BF16)
-    for j in range(width // HDIM):
-        lanes = cols(j)
-        pair = []
-        for side in range(2):
-            turn = turned(side, side, 1 - side)
-            pair.append(shift(
-                rim_send.at[side, :, lanes], rim_own.at[turn, :, lanes], rim_own.at[side, :, lanes],
-                rim_ssem.at[2 + side, j], rim_rsem.at[2 + turn, j], rim_rsem.at[2 + side, j], toward(side),
-            ))
-            pair[-1].start()
-        rims.append(pair)
-
-    for side in range(2):
-        queries[side].wait_recv()
-        queries[2 + side].start()
     totals = [spread_to(i, lsewin, lse_send, lse_recv) for i in range(4)]
     for copy in totals:
         copy.start()
@@ -316,46 +291,80 @@
 
     row = lax.broadcasted_iota(jnp.int32, (frames + 2 * HALF, HDIM), 0)
     inside = ((row >= HALF) | (c > 0)) & ((row < HALF + frames) | (c < count - 1))
-    spread = []
-
-    def take(j):
+    for j in range(width // HDIM):
         lanes = cols(j)
         for copy in parts[j]:
             copy.wait_recv()
         hidden = (own_sum[:, lanes] + part_recv[:, lanes].astype(F32)).astype(BF16)
         hpad[j, RIM : RIM + frames] = hidden.astype(F32)
-
-    take(0)
-    for j in range(width // HDIM):
-        if j + 1 < width // HDIM:
-            take(j + 1)
+        rim_send[0, :, lanes] = hidden[frames - RIM : frames]
+        rim_send[1, :, lanes] = hidden[0:RIM]
+    rims = []
+    for side in range(2):
+        turn = turned(side, side, 1 - side)
+        rims.append(shift(
+            rim_send.at[side], rim_own.at[turn], rim_own.at[side],
+            rim_ssem.at[side], rim_rsem.at[turn], rim_rsem.at[side], toward(side),
+        ))
+        rims[-1].start()
+
+    def conv_rows(j, start, rows):
         lanes = cols(j)
-        for copy in rims[j]:
-            copy.wait_recv()
-        low = (rim_own[0, :, lanes].astype(F32) + rim_far[0, :, lanes].astype(F32)).astype(BF16).astype(F32)
-        high = (rim_own[1, :, lanes].astype(F32) + rim_far[1, :, lanes].astype(F32)).astype(BF16).astype(F32)
-        hpad[j, 0:RIM] = jnp.where(c > 0, low, 0.0)
-        hpad[j, RIM + frames : 2 * RIM + frames] = jnp.where(c < count - 1, high, 0.0)
-        conv = jnp.zeros((frames + 2 * HALF, HDIM), F32)
+        conv = jnp.zeros((rows, HDIM), F32)
         for tap in range(ntaps):
-            conv = conv + taps[tap : tap + 1, lanes] * hpad[j, tap + 1 : tap + 1 + frames + 2 * HALF]
+            at = start + RIM - HALF + 1 + tap
+            conv = conv + taps[tap : tap + 1, lanes] * hpad[j, at : at + rows]
         gate = jax.nn.sigmoid(conv)
         swish = conv * gate
-        out_v[:, lanes] = (hpad[j, RIM : RIM + frames] + swish[HALF : HALF + frames]).astype(BF16)
-        cot = cotp[:, lanes].astype(F32)
+        low, high = max(start, 0), min(start + rows, frames)
+        out_v[low:high, lanes] = (
+            hpad[j, RIM + low : RIM + high] + swish[low - start : high - start]
+        ).astype(BF16)
+        span = slice(start + HALF, start + HALF + rows)
+        cot = cotp[span, lanes].astype(F32)
         grad_conv = (cot * (gate + swish * (1.0 - gate))).astype(BF16).astype(F32)
-        gpad[j] = jnp.where(inside, grad_conv, 0.0)
-        grad = cot[HALF : HALF + frames]
+        gpad[j, span] = jnp.where(inside[span], grad_conv, 0.0)
+
+    def grad_rows(j, start, rows):
+        lanes = cols(j)
+        grad = cotp[HALF + start : HALF + start + rows, lanes].astype(F32)
         for tap in range(ntaps):
-            start = 2 * HALF - 1 - tap
-            grad = grad + taps[tap : tap + 1, lanes] * gpad[j, start : start + frames]
-        gfull[0, :, lanes] = grad.astype(BF16)
-        to_sib = remote(gfull.at[0, :, lanes], gfull.at[1, :, lanes], gi_send.at[0, j], gi_recv.at[0, j], sib)
-        to_far = remote(gfull.at[0, :, lanes], gfull.at[2, :, lanes], gi_send.at[1, j], gi_recv.at[1, j], far)
-        relay = remote(gfull.at[2, :, lanes], gfull.at[3, :, lanes], gi_send.at[2, j], gi_recv.at[2, j], sib)
-        to_far.start()
-        to_sib.start()
-        spread.append((to_sib, to_far, relay))
+            at = start + 2 * HALF - 1 - tap
+            grad = grad + taps[tap : tap + 1, lanes] * gpad[j, at : at + rows]
+        gfull[0, start : start + rows, lanes] = grad.astype(BF16)
+
+    edges = ((0, RIM), (frames - RIM, RIM))
+    spans = (((RIM, frames - 2 * RIM),), edges)
+    spread = []
+
+    def leave(part, start, rows, lanes):
+        at, n = slice(start, start + rows), len(spread)
+        pieces = (
+            remote(gfull.at[0, at, lanes], gfull.at[1, at, lanes], gi_send.at[0, n], gi_recv.at[0, n], sib),
+            remote(gfull.at[0, at, lanes], gfull.at[2, at, lanes], gi_send.at[1, n], gi_recv.at[1, n], far),
+            remote(gfull.at[2, at, lanes], gfull.at[3, at, lanes], gi_send.at[2, n], gi_recv.at[2, n], sib),
+        )
+        pieces[1].start()
+        pieces[0].start()
+        spread.append((part,) + pieces)
+
+    for j in range(width // HDIM):
+        conv_rows(j, HALF, frames - 2 * HALF)
+        grad_rows(j, RIM, frames - 2 * RIM)
+        if j % 2 == 1:
+            leave(0, RIM, frames - 2 * RIM, slice((j - 1) * HDIM, (j + 1) * HDIM))
+    for copy in rims:
+        copy.wait_recv()
+    for j in range(width // HDIM):
+        lanes = cols(j)
+        hpad[j, 0:RIM] = jnp.where(c > 0, rim_own[0, :, lanes].astype(F32), 0.0)
+        hpad[j, RIM + frames : 2 * RIM + frames] = jnp.where(c < count - 1, rim_own[1, :, lanes].astype(F32), 0.0)
+        conv_rows(j, -HALF, 2 * HALF)
+        conv_rows(j, frames - HALF, 2 * HALF)
+        for start, rows in edges:
+            grad_rows(j, start, rows)
+    for start, rows in edges:
+        leave(1, start, rows, slice(0, width))
 
     stores = [
         pltpu.make_async_copy(out_v, out_hbm, out_sem.at[0]),
@@ -364,50 +373,66 @@
     for copy in stores:
         copy.start()
 
-    for copy in queries[2:] + totals:
-        copy.wait_recv()
-    for h in range(heads):
-        scores_t = nt(kwin[h, mid], qwin[h]) * scale
-        probs_t[h] = jnp.where(valid, jnp.exp(scores_t - lsewin[h : h + 1]), 0.0)
-
-    up = nt(gfull[0], w_own[:, wide(m)])
-    for to_sib, to_far, relay in spread:
-        to_far.wait_recv()
-        relay.start()
-    for to_sib, to_far, relay in spread:
+    for side in range(2):
+        queries[side].wait_recv()
+        queries[2 + side].start()
+
+    own_up = nt(gfull[0], w_own[:, wide(m)])
+    for _, to_sib, _, _ in spread:
         to_sib.wait_recv()
-    up = up + nt(gfull[1], w_own[:, wide(sib_m)])
-    up = up + nt(gfull[2], w_own[:, wide(far_m)])
-    for to_sib, to_far, relay in spread:
-        relay.wait_recv()
-    up = up + nt(gfull[3], w_own[:, wide(far_sib_m)])
-    upstream = up.astype(BF16)
+    own_up = own_up + nt(gfull[1], w_own[:, wide(sib_m)])
+    ups = []
+    second_ups = []
+    def rows_of(take, part):
+        pieces = [take(slice(start, start + rows)) for start, rows in spans[part]]
+        return pieces[0] if len(pieces) == 1 else jnp.concatenate(pieces, axis=0)
+
+    for r in range(2):
+        mine = [piece for piece in spread if piece[0] == r]
+        for _, _, to_far, relay in mine:
+            to_far.wait_recv()
+            relay.start()
+        up = rows_of(lambda at: own_up[at], r) + nt(rows_of(lambda at: gfull[2, at], r), w_own[:, wide(far_m)])
+        for _, _, _, relay in mine:
+            relay.wait_recv()
+        up = up + nt(rows_of(lambda at: gfull[3, at], r), w_own[:, wide(far_sib_m)])
+        upstream = up.astype(BF16)
+        begun = 0
+        for start, rows in spans[r]:
+            for h in range(heads):
+                dowin[h, LOOK * frames + start : LOOK * frames + start + rows] = upstream[begun : begun + rows, cols(h)]
+            begun += rows
+
+        for start, rows in spans[r]:
+            n = len(ups) // 2
+
+            def rows_at(slot, start=start, rows=rows):
+                return pl.ds(pl.multiple_of(slot * frames + start, RIM), rows)
+
+            for side in range(2):
+                turn = turned(side, side, 1 - side)
+                near_slot, far_slot = places[side], places[2 + side]
+                own_at, near_at, far_at = rows_at(LOOK), rows_at(near_slot), rows_at(far_slot)
+                near_to = rows_at(turned(side, near_slot, 4 - near_slot))
+                far_to = rows_at(turned(side, far_slot, 4 - far_slot))
+                ups.append(shift(
+                    dowin.at[:, own_at], dowin.at[:, near_to], dowin.at[:, near_at],
+                    do_send.at[side, n], do_recv.at[turn, n], do_recv.at[side, n], toward(side),
+                ))
+                ups[-1].start()
+                second_ups.append(shift(
+                    dowin.at[:, near_at], dowin.at[:, far_to], dowin.at[:, far_at],
+                    do_send.at[2 + side, n], do_recv.at[2 + turn, n], do_recv.at[2 + side, n], toward(side),
+                ))
 
     delta = []
     stat = jnp.zeros((frames, HDIM), F32)
     for h in range(heads):
-        part = upstream[:, cols(h)]
-        dowin[h, mid] = part
         delta.append(
-            jnp.sum(part.astype(F32) * att[0, :, cols(h)].astype(F32), axis=1, keepdims=True)
+            jnp.sum(dowin[h, mid].astype(F32) * att[0, :, cols(h)].astype(F32), axis=1, keepdims=True)
         )
         stat = jnp.where(lane == h, delta[h], stat)
     deltawin[:, mid] = jnp.transpose(stat)[0:8]
-    ups = []
-    second_ups = []
-    for h in range(heads):
-        for side in range(2):
-            turn = turned(side, side, 1 - side)
-            near_slot, far_slot = places[side], places[2 + side]
-            ups.append(shift(
-                dowin.at[h, mid], dowin.at[h, place(side, near_slot)], dowin.at[h, block(near_slot)],
-                do_send.at[side, h], do_recv.at[turn, h], do_recv.at[side, h], toward(side),
-            ))
-            ups[-1].start()
-            second_ups.append(shift(
-                dowin.at[h, block(near_slot)], dowin.at[h, place(side, far_slot)], dowin.at[h, block(far_slot)],
-                do_send.at[2 + side, h], do_recv.at[2 + turn, h], do_recv.at[2 + side, h], toward(side),
-            ))
     deltas = [spread_to(i, deltawin, delta_send, delta_recv) for i in range(4)]
     for copy in deltas:
         copy.start()
@@ -433,12 +458,18 @@
         two.start()
     for copy in deltas:
         copy.wait_recv()
+
+    for copy in queries[2:] + totals:
+        copy.wait_recv()
+    for h in range(heads):
+        scores_t = nt(kwin[h, mid], qwin[h]) * scale
+        probs_t[h] = jnp.where(valid, jnp.exp(scores_t - lsewin[h : h + 1]), 0.0)
     near = slice(frames, 4 * frames)
     for h in range(heads):
         gk_sum[:, cols(h)], gv_sum[:, cols(h)] = key_grad(h, near)
-    for h in range(heads):
-        for side in range(2):
-            second_ups[2 * h + side].wait_recv()
+    for copy in second_ups:
+        copy.wait_recv()
+    for h in range(heads):
         low_k, low_v = key_grad(h, block(0))
         high_k, high_v = key_grad(h, block(4))
         gk_v[:, cols(h)] = (gk_sum[:, cols(h)] + low_k + high_k).astype(BF16)
@@ -452,7 +483,7 @@
         copy.wait_send()
     for copy in ups + second_ups + deltas:
         copy.wait_send()
-    for group in parts + rims + spread:
+    for group in parts + [rims] + [piece[1:] for piece in spread]:
         for copy in group:
             copy.wait_send()
     for copy in stores:
@@ -499,7 +530,6 @@
         pltpu.VMEM((frames, width), BF16),
         pltpu.VMEM((2, RIM, width), BF16),
         pltpu.VMEM((2, RIM, width), BF16),
-        pltpu.VMEM((2, RIM, width), BF16),
         pltpu.VMEM((chunks, frames + 2 * RIM, HDIM), F32),
         pltpu.VMEM((chunks, frames + 2 * HALF, HDIM), F32),
         pltpu.VMEM((4, frames, width), BF16),
@@ -520,8 +550,8 @@
         dma((2,)), dma((2,)),
         dma((heads,)), dma((heads,)),
         dma((chunks,)), dma((chunks,)),
-        dma((4, chunks)), dma((4, chunks)),
-        dma((3, chunks)), dma((3, chunks)),
+        dma((2,)), dma((2,)),
+        dma((3, 4)), dma((3, 4)),
     ]
     shape = jax.ShapeDtypeStruct((frames, width), BF16)
     results = pl.pallas_call(

time: 72.4 us -> 71.5 us (0.988)
  Pallas kernels: 71.5 us -> 70.7 us
where the time goes in v3:
time: 71.5 us; the launch traced here: 71.4 us
  Pallas kernels  70.7 us (99%)
    pallas_call x1, Pallas kernels, per_device(): pl.pallas_call(functools.partial(kernel_body, count, heads), out_shape=(s...  68.8 us
    pallas_call x1, Pallas kernels, per_device(): pl.pallas_call(copy_out, out_shape=(shape,) * 5, in_specs=[pl.BlockSpec(m...  1.91 us

profile of v3, /device:TPU:9, one launch (start us, length us, event | category | flops | bytes accessed | tf_op | source)
XLA Modules:
  0.0 71.4 jit_solution(7164972407247418715)
XLA Ops:
  0.6 68.8 %conformer.1 = (bf16[128,512]{1,0:T(8,128)(2,1)}, bf16[128,512]{1,0:T(8,128)(2,1)}, bf16[128,512]{1,0:T(8,128)(2,1)}, bf16[128,512]{1,0:T(8,128)(2,1)}, bf16[128,512]{1,0:T(8,128)(2,1)}) custom-call(bf16[128,512]{1,0:T(8,128)(2,1)} %q_hbm.1, bf16[128,512]{1,0:T(8,128)(2,1)} %k_hbm.1, bf16[128,512]{1,0:T(8,128)(2,1)} %v_hbm.1, bf16[128,512]{1,0:T(8,128)(2,1)} %in_hbm.1, ...), custom_call_target="tpu_custom_call" | custom-call | tf_op jit(solution)/shard_map/conformer/pallas_call | solution.py:557
  69.5 1.9 %copy_out.1 = (bf16[128,512]{1,0:T(8,128)(2,1)}, bf16[128,512]{1,0:T(8,128)(2,1)}, bf16[128,512]{1,0:T(8,128)(2,1)}, bf16[128,512]{1,0:T(8,128)(2,1)}, bf16[128,512]{1,0:T(8,128)(2,1)}) custom-call(bf16[128,512]{1,0:T(8,128)(2,1)} %get-tuple-element.10.refs_0_, bf16[128,512]{1,0:T(8,128)(2,1)} %get-tuple-element.11.refs_1_, ...), custom_call_target="tpu_custom_call" | custom-call | tf_op jit(solution)/shard_map/copy_out/pallas_call | solution.py:568

commit v4 on v3

--- a/solution.py
+++ b/solution.py
@@ -159,17 +159,6 @@
         return pl.ds(pl.multiple_of(index * width, width), width)
 
     mid = block(LOOK)
-    loads = {}
-    for h in range(heads):
-        loads["q", h] = local(q_hbm.at[:, cols(h)], qwin.at[h, mid], h)
-        loads["k", h] = local(k_hbm.at[:, cols(h)], kwin.at[h, mid], heads + h)
-        loads["v", h] = local(v_hbm.at[:, cols(h)], vwin.at[h, mid], 2 * heads + h)
-    at = 3 * heads
-    loads["w"] = local(w_hbm, w_own, at)
-    loads["taps"] = local(tap_hbm, taps, at + 1)
-    loads["inp"] = local(in_hbm, inp, at + 2)
-    loads["cot"] = local(cot_hbm, cotp.at[HALF : HALF + frames], at + 3)
-
     pl.semaphore_wait(barrier, len(partners))
 
     first = {}
@@ -202,6 +191,17 @@
             cotp.at[cot_starts[side] : cot_starts[side] + HALF],
             cot_send.at[side], cot_recv.at[turned(side, side, 1 - side)], cot_recv.at[side], toward(side),
         ))
+    loads = {}
+    for h in range(heads):
+        loads["q", h] = local(q_hbm.at[:, cols(h)], qwin.at[h, mid], h)
+        loads["k", h] = local(k_hbm.at[:, cols(h)], kwin.at[h, mid], heads + h)
+        loads["v", h] = local(v_hbm.at[:, cols(h)], vwin.at[h, mid], 2 * heads + h)
+    at = 3 * heads
+    loads["w"] = local(w_hbm, w_own, at)
+    loads["taps"] = local(tap_hbm, taps, at + 1)
+    loads["inp"] = local(in_hbm, inp, at + 2)
+    loads["cot"] = local(cot_hbm, cotp.at[HALF : HALF + frames], at + 3)
+
     for h in range(heads):
         for side in range(2):
             for i in range(2):
@@ -257,9 +257,10 @@
         share = remote(att.at[0, :, cols(h)], att.at[1, :, cols(h)], att_send.at[h], att_recv.at[h], sib)
         share.start()
         shares.append(share)
+
+    loads["w"].wait()
+    far_part = nn(att[0], w_own[:, wide(far_m)])
     lsewin[:, mid] = jnp.transpose(stat)[0:8]
-
-    loads["w"].wait()
     early[0].wait_recv()
     early[1].wait_recv()
     for share in shares:
@@ -267,8 +268,7 @@
     parts = []
     for j in range(width // HDIM):
         lanes = cols(j)
-        far_cols = pl.ds(pl.multiple_of(far_m * width + j * HDIM, HDIM), HDIM)
-        part_send[:, lanes] = (nn(att[0], w_own[:, far_cols]) + nn(att[1], w_sib[1, :, lanes])).astype(BF16)
+        part_send[:, lanes] = (far_part[:, lanes] + nn(att[1], w_sib[1, :, lanes])).astype(BF16)
         group = [
             remote(part_send.at[:, lanes], part_recv.at[:, lanes], part_ssem.at[j], part_rsem.at[j], far)
         ]
@@ -377,10 +377,6 @@
         queries[side].wait_recv()
         queries[2 + side].start()
 
-    own_up = nt(gfull[0], w_own[:, wide(m)])
-    for _, to_sib, _, _ in spread:
-        to_sib.wait_recv()
-    own_up = own_up + nt(gfull[1], w_own[:, wide(sib_m)])
     ups = []
     second_ups = []
     def rows_of(take, part):
@@ -389,10 +385,14 @@
 
     for r in range(2):
         mine = [piece for piece in spread if piece[0] == r]
+        up = nt(rows_of(lambda at: gfull[0, at], r), w_own[:, wide(m)])
+        for _, to_sib, _, _ in mine:
+            to_sib.wait_recv()
+        up = up + nt(rows_of(lambda at: gfull[1, at], r), w_own[:, wide(sib_m)])
         for _, _, to_far, relay in mine:
             to_far.wait_recv()
             relay.start()
-        up = rows_of(lambda at: own_up[at], r) + nt(rows_of(lambda at: gfull[2, at], r), w_own[:, wide(far_m)])
+        up = up + nt(rows_of(lambda at: gfull[2, at], r), w_own[:, wide(far_m)])
         for _, _, _, relay in mine:
             relay.wait_recv()
         up = up + nt(rows_of(lambda at: gfull[3, at], r), w_own[:, wide(far_sib_m)])
@@ -420,10 +420,19 @@
                     do_send.at[side, n], do_recv.at[turn, n], do_recv.at[side, n], toward(side),
                 ))
                 ups[-1].start()
+                if r == 0:
+                    second_ups.append(shift(
+                        dowin.at[:, near_at], dowin.at[:, far_to], dowin.at[:, far_at],
+                        do_send.at[2 + side, n], do_recv.at[2 + turn, n], do_recv.at[2 + side, n], toward(side),
+                    ))
+                    continue
+                over = 2 + side
+                far_to = rows_at(turned(over, far_slot, 4 - far_slot))
                 second_ups.append(shift(
-                    dowin.at[:, near_at], dowin.at[:, far_to], dowin.at[:, far_at],
-                    do_send.at[2 + side, n], do_recv.at[2 + turn, n], do_recv.at[2 + side, n], toward(side),
+                    dowin.at[:, own_at], dowin.at[:, far_to], dowin.at[:, far_at],
+                    do_send.at[over, n], do_recv.at[turned(over, over, over ^ 1), n], do_recv.at[over, n], toward(over),
                 ))
+                second_ups[-1].start()
 
     delta = []
     stat = jnp.zeros((frames, HDIM), F32)
@@ -453,9 +462,10 @@
         query_grad(h)
     stores.append(pltpu.make_async_copy(gq_v, gq_hbm, out_sem.at[2]))
     stores[-1].start()
-    for one, two in zip(ups, second_ups):
+    for n, (one, two) in enumerate(zip(ups, second_ups)):
         one.wait_recv()
-        two.start()
+        if n < 2:
+            two.start()
     for copy in deltas:
         copy.wait_recv()
 
@@ -492,8 +502,14 @@
 
 def copy_out(*refs):
     sources, targets, held, sems = refs[:5], refs[5:10], refs[10], refs[11]
-    taken = [pltpu.make_async_copy(source, held.at[i], sems.at[0, i]) for i, source in enumerate(sources)]
-    given = [pltpu.make_async_copy(held.at[i], target, sems.at[1, i]) for i, target in enumerate(targets)]
+    half = held.shape[1] // 2
+    cuts = [(i, slice(j * half, (j + 1) * half)) for i in range(5) for j in range(2)]
+    taken = [
+        pltpu.make_async_copy(sources[i].at[at], held.at[i, at], sems.at[0, n]) for n, (i, at) in enumerate(cuts)
+    ]
+    given = [
+        pltpu.make_async_copy(held.at[i, at], targets[i].at[at], sems.at[1, n]) for n, (i, at) in enumerate(cuts)
+    ]
     for copy in taken:
         copy.start()
     for one, two in zip(taken, given):
@@ -570,7 +586,7 @@
         out_shape=(shape,) * 5,
         in_specs=[pl.BlockSpec(memory_space=pl.ANY)] * 5,
         out_specs=(pl.BlockSpec(memory_space=pl.ANY),) * 5,
-        scratch_shapes=[pltpu.VMEM((5, frames, width), BF16), dma((2, 5))],
+        scratch_shapes=[pltpu.VMEM((5, frames, width), BF16), dma((2, 10))],
         compiler_params=pltpu.CompilerParams(vmem_limit_bytes=56 * 1024 * 1024),
         name="copy_out",
     )(*results)

time: 71.5 us -> 69.5 us (0.972)
  Pallas kernels: 70.7 us -> 68.7 us
    pallas_call x1, Pallas kernels: 68.8 us -> 66.7 us  [per_device(): pl.pallas_call(functools.partial(kernel_body, count, heads), out_shape=(s...]
where the time goes in v4:
time: 69.5 us; the launch traced here: 69.3 us
  Pallas kernels  68.7 us (99%)
    pallas_call x1, Pallas kernels, per_device(): pl.pallas_call(functools.partial(kernel_body, count, heads), out_shape=(s...  66.7 us
    pallas_call x1, Pallas kernels, per_device(): pl.pallas_call(copy_out, out_shape=(shape,) * 5, in_specs=[pl.BlockSpec(m...  1.92 us

profile of v4, /device:TPU:9, one launch (start us, length us, event | category | flops | bytes accessed | tf_op | source)
XLA Modules:
  0.0 69.3 jit_solution(7435886795910329436)
XLA Ops:
  0.6 66.7 %conformer.1 = (bf16[128,512]{1,0:T(8,128)(2,1)}, bf16[128,512]{1,0:T(8,128)(2,1)}, bf16[128,512]{1,0:T(8,128)(2,1)}, bf16[128,512]{1,0:T(8,128)(2,1)}, bf16[128,512]{1,0:T(8,128)(2,1)}) custom-call(bf16[128,512]{1,0:T(8,128)(2,1)} %q_hbm.1, bf16[128,512]{1,0:T(8,128)(2,1)} %k_hbm.1, bf16[128,512]{1,0:T(8,128)(2,1)} %v_hbm.1, bf16[128,512]{1,0:T(8,128)(2,1)} %in_hbm.1, ...), custom_call_target="tpu_custom_call" | custom-call | tf_op jit(solution)/shard_map/conformer/pallas_call | solution.py:573
  67.4 1.9 %copy_out.1 = (bf16[128,512]{1,0:T(8,128)(2,1)}, bf16[128,512]{1,0:T(8,128)(2,1)}, bf16[128,512]{1,0:T(8,128)(2,1)}, bf16[128,512]{1,0:T(8,128)(2,1)}, bf16[128,512]{1,0:T(8,128)(2,1)}) custom-call(bf16[128,512]{1,0:T(8,128)(2,1)} %get-tuple-element.10.refs_0_, bf16[128,512]{1,0:T(8,128)(2,1)} %get-tuple-element.11.refs_1_, ...), custom_call_target="tpu_custom_call" | custom-call | tf_op jit(solution)/shard_map/copy_out/pallas_call | solution.py:584

commit v5 on v4

--- a/solution.py
+++ b/solution.py
@@ -173,6 +173,15 @@
                     kv_recv.at[side, i, h], toward(side),
                 )
                 first[h, i, side].start()
+                if h == heads - 1:
+                    over = 2 + side
+                    second[h, i, side] = shift(
+                        src.at[:, cols(h)], win.at[h, place(over, far_slot)], win.at[h, block(far_slot)],
+                        kv_send.at[over, i, h], kv_recv.at[turned(over, over, over ^ 1), i, h],
+                        kv_recv.at[over, i, h], toward(over),
+                    )
+                    second[h, i, side].start()
+                    continue
                 second[h, i, side] = shift(
                     win.at[h, block(near_slot)], win.at[h, place(side, far_slot)], win.at[h, block(far_slot)],
                     kv_send.at[2 + side, i, h], kv_recv.at[2 + turned(side, side, 1 - side), i, h],
@@ -206,7 +215,8 @@
         for side in range(2):
             for i in range(2):
                 first[h, i, side].wait_recv()
-                second[h, i, side].start()
+                if h < heads - 1:
+                    second[h, i, side].start()
 
     for copy in early:
         copy.start()

time: 69.5 us -> 71.2 us (1.024)
  Pallas kernels: 68.7 us -> 70.4 us
    pallas_call x1, Pallas kernels: 66.7 us -> 68.4 us  [per_device(): pl.pallas_call(functools.partial(kernel_body, count, heads), out_shape=(s...]
where the time goes in v5:
time: 71.2 us; the launch traced here: 71 us
  Pallas kernels  70.4 us (99%)
    pallas_call x1, Pallas kernels, per_device(): pl.pallas_call(functools.partial(kernel_body, count, heads), out_shape=(s...  68.4 us
    pallas_call x1, Pallas kernels, per_device(): pl.pallas_call(copy_out, out_shape=(shape,) * 5, in_specs=[pl.BlockSpec(m...  1.92 us

profile of v5, /device:TPU:9, one launch (start us, length us, event | category | flops | bytes accessed | tf_op | source)
XLA Modules:
  0.0 71.0 jit_solution(1904162440729972719)
XLA Ops:
  0.6 68.4 %conformer.1 = (bf16[128,512]{1,0:T(8,128)(2,1)}, bf16[128,512]{1,0:T(8,128)(2,1)}, bf16[128,512]{1,0:T(8,128)(2,1)}, bf16[128,512]{1,0:T(8,128)(2,1)}, bf16[128,512]{1,0:T(8,128)(2,1)}) custom-call(bf16[128,512]{1,0:T(8,128)(2,1)} %q_hbm.1, bf16[128,512]{1,0:T(8,128)(2,1)} %k_hbm.1, bf16[128,512]{1,0:T(8,128)(2,1)} %v_hbm.1, bf16[128,512]{1,0:T(8,128)(2,1)} %in_hbm.1, ...), custom_call_target="tpu_custom_call" | custom-call | tf_op jit(solution)/shard_map/conformer/pallas_call | solution.py:583
  69.1 1.9 %copy_out.1 = (bf16[128,512]{1,0:T(8,128)(2,1)}, bf16[128,512]{1,0:T(8,128)(2,1)}, bf16[128,512]{1,0:T(8,128)(2,1)}, bf16[128,512]{1,0:T(8,128)(2,1)}, bf16[128,512]{1,0:T(8,128)(2,1)}) custom-call(bf16[128,512]{1,0:T(8,128)(2,1)} %get-tuple-element.10.refs_0_, bf16[128,512]{1,0:T(8,128)(2,1)} %get-tuple-element.11.refs_1_, ...), custom_call_target="tpu_custom_call" | custom-call | tf_op jit(solution)/shard_map/copy_out/pallas_call | solution.py:594
